TPU v7x, 32 devices: a whole 2x2x4 slice. The times are simulated.
32 devices in a mesh: dp: 16 (over z, y, x), grp: 2 (over core).
Axes of the slice: x: 2, y: 2, z: 4, core: 2. Of those that a mesh axis runs over, the one named last changes fastest.
Arguments:
- tokens: bfloat16 [32, 512, 1152], P('dp', 'grp'), may hold values from -6 to 6
- cotangent: bfloat16 [32, 512, 1152], P('dp', 'grp'), may hold values from -6 to 6
- condition: float32 [24, 1152], P(None, 'dp'), may hold values from -6 to 6
- latent_of: int32 [32], P('dp'), may hold values from 0 to 23, as said below
- slot_valid: int32 [32], P('dp'), may hold values from 0 to 1, as said below
- ada_weight: float32 [1152, 6912], P('dp', 'grp'), may hold values from -0.1875 to 0.1875
- ada_weight_mean: float32 [1152, 6912], P('dp', 'grp'), may hold values from -0.03125 to 0.03125
- ada_weight_square: float32 [1152, 6912], P('dp', 'grp'), may hold values from 2e-06 to 1e-05
- ada_offset: float32 [6912], P('grp'), may hold values from -0.75 to 0.75
- ada_offset_mean: float32 [6912], P('grp'), may hold values from -0.03125 to 0.03125
- ada_offset_square: float32 [6912], P('grp'), may hold values from 2e-06 to 1e-05
- qkv_weight: float32 [1152, 3456], P('dp', 'grp'), may hold values from -0.1875 to 0.1875
- qkv_weight_mean: float32 [1152, 3456], P('dp', 'grp'), may hold values from -0.03125 to 0.03125
- qkv_weight_square: float32 [1152, 3456], P('dp', 'grp'), may hold values from 2e-06 to 1e-05
- proj_weight: float32 [1152, 1152], P('dp', 'grp'), may hold values from -0.5 to 0.5
- proj_weight_mean: float32 [1152, 1152], P('dp', 'grp'), may hold values from -0.03125 to 0.03125
- proj_weight_square: float32 [1152, 1152], P('dp', 'grp'), may hold values from 2e-06 to 1e-05
- up_weight: float32 [1152, 4608], P('dp', 'grp'), may hold values from -1 to 1
- up_weight_mean: float32 [1152, 4608], P('dp', 'grp'), may hold values from -0.03125 to 0.03125
- up_weight_square: float32 [1152, 4608], P('dp', 'grp'), may hold values from 2e-06 to 1e-05
- down_weight: float32 [4608, 1152], P('dp', 'grp'), may hold values from -0.375 to 0.375
- down_weight_mean: float32 [4608, 1152], P('dp', 'grp'), may hold values from -0.03125 to 0.03125
- down_weight_square: float32 [4608, 1152], P('dp', 'grp'), may hold values from 2e-06 to 1e-05
- main_bias: float32 [9216], P(('dp', 'grp')), may hold values from -0.75 to 0.75
- main_bias_mean: float32 [9216], P(('dp', 'grp')), may hold values from -0.03125 to 0.03125
- main_bias_square: float32 [9216], P(('dp', 'grp')), may hold values from 2e-06 to 1e-05
Outputs:
- block_out: bfloat16 [32, 512, 1152], P('dp', 'grp')
- tokens_grad: bfloat16 [32, 512, 1152], P('dp', 'grp')
- condition_grad: float32 [24, 1152], P(None, 'dp')
- ada_weight_grad: float32 [1152, 6912], P('dp', 'grp')
- ada_weight_new: float32 [1152, 6912], P('dp', 'grp')
- ada_weight_mean_new: float32 [1152, 6912], P('dp', 'grp')
- ada_weight_square_new: float32 [1152, 6912], P('dp', 'grp')
- ada_offset_grad: float32 [6912], P('grp')
- ada_offset_new: float32 [6912], P('grp')
- ada_offset_mean_new: float32 [6912], P('grp')
- ada_offset_square_new: float32 [6912], P('grp')
- qkv_weight_grad: float32 [1152, 3456], P('dp', 'grp')
- qkv_weight_new: float32 [1152, 3456], P('dp', 'grp')
- qkv_weight_mean_new: float32 [1152, 3456], P('dp', 'grp')
- qkv_weight_square_new: float32 [1152, 3456], P('dp', 'grp')
- proj_weight_grad: float32 [1152, 1152], P('dp', 'grp')
- proj_weight_new: float32 [1152, 1152], P('dp', 'grp')
- proj_weight_mean_new: float32 [1152, 1152], P('dp', 'grp')
- proj_weight_square_new: float32 [1152, 1152], P('dp', 'grp')
- up_weight_grad: float32 [1152, 4608], P('dp', 'grp')
- up_weight_new: float32 [1152, 4608], P('dp', 'grp')
- up_weight_mean_new: float32 [1152, 4608], P('dp', 'grp')
- up_weight_square_new: float32 [1152, 4608], P('dp', 'grp')
- down_weight_grad: float32 [4608, 1152], P('dp', 'grp')
- down_weight_new: float32 [4608, 1152], P('dp', 'grp')
- down_weight_mean_new: float32 [4608, 1152], P('dp', 'grp')
- down_weight_square_new: float32 [4608, 1152], P('dp', 'grp')
- main_bias_grad: float32 [9216], P(('dp', 'grp'))
- main_bias_new: float32 [9216], P(('dp', 'grp'))
- main_bias_mean_new: float32 [9216], P(('dp', 'grp'))
- main_bias_square_new: float32 [9216], P(('dp', 'grp'))
Inputs may be any that keep to these rules, and one draw needn't show every extreme that they name: `slot_valid`: each index of dp has 2 slots; some index of dp has all 2 valid; exactly 24 slots are valid in all. `latent_of`: the valid slots name each of the 24 latents exactly once; a padding slot names some latent and is ignored.
All inputs are finite; a program needn't handle non-finite values.
Results may differ from a plain program's by a relative error of at most 0.024.
Values may be sent and summed in bfloat16 or wider, within the bound.
A program may use at most 256 MiB of HBM per device.

v0:
```python
import math

import jax
import jax.numpy as jnp
from jax import lax
from jax.sharding import PartitionSpec as P

D = 1152
HD = 72
HEADS = 16
FF = 4608
HW = 1152


eps_norm = 1e-06
beta_one = 0.9
beta_two = 0.95
learn_rate = 0.015
decay_rate = 0.01
adam_eps = 1e-08
clip_rms = 0.01
clip_eps = 1e-06
step_count = 10
gelu_coef = 0.7978845608028654
cubic_term = 0.044715
highest = lax.Precision.HIGHEST


def contract(pattern, left, right):
    return jnp.einsum(pattern, left, right, preferred_element_type=jnp.float32)


def gelu_forward(values):
    inside = gelu_coef * (values + cubic_term * values * values * values)
    return 0.5 * values * (1.0 + jnp.tanh(inside))


def gelu_slope(values):
    inside = gelu_coef * (values + cubic_term * values * values * values)
    tangent = jnp.tanh(inside)
    return 0.5 * (1.0 + tangent) + 0.5 * values * (1.0 - tangent * tangent) * gelu_coef * (
        1.0 + 3.0 * cubic_term * values * values
    )


def layer_norm(values):
    centred = values - jnp.mean(values, axis=-1, keepdims=True)
    inv_std = lax.rsqrt(jnp.mean(centred * centred, axis=-1, keepdims=True) + eps_norm)
    return (centred * inv_std, inv_std)


def norm_back(grad_normed, normed, inv_std):
    return inv_std * (
        grad_normed
        - jnp.mean(grad_normed, axis=-1, keepdims=True)
        - normed * jnp.mean(grad_normed * normed, axis=-1, keepdims=True)
    )


def adam_update(weight, first_mom, second_mom, gradient, factor):
    clipped = gradient * factor
    first_new = beta_one * first_mom + (1.0 - beta_one) * clipped
    second_new = beta_two * second_mom + (1.0 - beta_two) * clipped * clipped
    corr_one = 1.0 - beta_one**step_count
    corr_two = 1.0 - beta_two**step_count
    direction = first_new / corr_one / (jnp.sqrt(second_new / corr_two) + adam_eps)
    weight_new = weight - learn_rate * (direction + decay_rate * weight)
    return (weight_new, first_new, second_new)


def clip_from(total, count):
    return jnp.minimum(1.0, clip_rms * lax.rsqrt(total / count + clip_eps))


def split_heads(values):
    return values.reshape(values.shape[:-1] + (HEADS, HD))


def reduce_bucket(first_grad, second_grad, bias_grad):
    bias_rows = bias_grad.reshape(lax.axis_size("dp"), -1)
    summed = (
        lax.psum_scatter(
            first_grad.astype(jnp.bfloat16), "dp", scatter_dimension=0, tiled=True
        ).astype(jnp.float32),
        lax.psum_scatter(
            second_grad.astype(jnp.bfloat16), "dp", scatter_dimension=0, tiled=True
        ).astype(jnp.float32),
        lax.psum_scatter(
            bias_rows.astype(jnp.bfloat16), "dp", scatter_dimension=0, tiled=True
        ).astype(jnp.float32),
    )
    owned = (
        lax.psum_scatter(
            summed[0].astype(jnp.bfloat16), "grp", scatter_dimension=1, tiled=True
        ).astype(jnp.float32),
        lax.psum_scatter(
            summed[1].astype(jnp.bfloat16), "grp", scatter_dimension=1, tiled=True
        ).astype(jnp.float32),
        lax.psum_scatter(
            summed[2].astype(jnp.bfloat16), "grp", scatter_dimension=1, tiled=True
        ).astype(jnp.float32),
    )
    return (owned[0], owned[1], owned[2].reshape(-1))


def local(
    tokens,
    cotangent,
    condition,
    latent_of,
    slot_valid,
    ada_weight,
    ada_weight_mean,
    ada_weight_square,
    ada_offset,
    ada_offset_mean,
    ada_offset_square,
    qkv_weight,
    qkv_weight_mean,
    qkv_weight_square,
    proj_weight,
    proj_weight_mean,
    proj_weight_square,
    up_weight,
    up_weight_mean,
    up_weight_square,
    down_weight,
    down_weight_mean,
    down_weight_square,
    main_bias,
    main_bias_mean,
    main_bias_square,
):
    latents = condition.shape[0]
    slot_count = tokens.shape[0]
    scale_dot = 1.0 / math.sqrt(HD)
    qkv_part, proj_part, up_part, down_part, bias_part = (
        lax.all_gather(qkv_weight.astype(jnp.bfloat16), "grp", axis=1, tiled=True),
        lax.all_gather(proj_weight.astype(jnp.bfloat16), "grp", axis=1, tiled=True),
        lax.all_gather(up_weight.astype(jnp.bfloat16), "grp", axis=1, tiled=True),
        lax.all_gather(down_weight.astype(jnp.bfloat16), "grp", axis=1, tiled=True),
        lax.all_gather(main_bias.astype(jnp.bfloat16), "grp", axis=0, tiled=True),
    )
    qkv_full, proj_full, up_full, down_full, bias_full = (
        lax.all_gather(qkv_part, "dp", axis=0, tiled=True),
        lax.all_gather(proj_part, "dp", axis=0, tiled=True),
        lax.all_gather(up_part, "dp", axis=0, tiled=True),
        lax.all_gather(down_part, "dp", axis=0, tiled=True),
        lax.all_gather(bias_part, "dp", axis=0, tiled=True),
    )
    bias_float = bias_full.astype(jnp.float32)
    bias_query = bias_float[:HW]
    bias_value = bias_float[HW : 2 * HW]
    bias_proj = bias_float[2 * HW : 2 * HW + D]
    bias_up = bias_float[2 * HW + D : 2 * HW + D + FF]
    bias_down = bias_float[2 * HW + D + FF :]
    silu_cond = jax.nn.silu(condition)
    col_width = ada_weight.shape[1]
    first_data = jnp.where(lax.axis_index("dp") == 0, 1.0, 0.0).astype(jnp.float32)
    mod_piece = jnp.dot(silu_cond, ada_weight, precision=highest) + first_data * ada_offset
    mod_spread = lax.dynamic_update_slice_in_dim(
        jnp.zeros((latents, 6 * D), jnp.float32), mod_piece, lax.axis_index("grp") * col_width, 1
    )
    mod_table = lax.psum(mod_spread, ("dp", "grp"))
    slot_pick = (latent_of[:, None] == jnp.arange(latents, dtype=jnp.int32)[None, :]).astype(
        jnp.float32
    )
    slot_mod = jnp.dot(slot_pick, mod_table, precision=highest)[:, None, :]
    shift_one = slot_mod[..., :D]
    scale_one = slot_mod[..., D : 2 * D]
    gate_one = slot_mod[..., 2 * D : 3 * D]
    shift_two = slot_mod[..., 3 * D : 4 * D]
    scale_two = slot_mod[..., 4 * D : 5 * D]
    gate_two = slot_mod[..., 5 * D :]
    slot_keep = slot_valid.astype(jnp.float32)[:, None, None]
    tok_float = tokens.astype(jnp.float32)
    normed_one, inv_one = layer_norm(tok_float)
    hidden_one = (normed_one * (1.0 + scale_one) + shift_one).astype(jnp.bfloat16)
    projected = contract("std,de->ste", hidden_one, qkv_full)
    queries = (projected[..., :HW] + bias_query).astype(jnp.bfloat16)
    keys_own = projected[..., HW : 2 * HW].astype(jnp.bfloat16)
    values_own = (projected[..., 2 * HW :] + bias_value).astype(jnp.bfloat16)
    keys_all, values_all = (
        lax.all_gather(keys_own, "grp", axis=1, tiled=True),
        lax.all_gather(values_own, "grp", axis=1, tiled=True),
    )
    query_heads = split_heads(queries)
    key_heads = split_heads(keys_all)
    value_heads = split_heads(values_all)
    scores = contract("sqhd,skhd->shqk", query_heads, key_heads) * scale_dot
    row_max = jnp.max(scores, axis=-1, keepdims=True)
    log_total = row_max + jnp.log(jnp.sum(jnp.exp(scores - row_max), axis=-1, keepdims=True))
    probs_half = jnp.exp(scores - log_total).astype(jnp.bfloat16)
    attended = (
        contract("shqk,skhd->sqhd", probs_half, value_heads)
        .astype(jnp.bfloat16)
        .reshape(queries.shape)
    )
    branch = contract("ste,ed->std", attended, proj_full) + bias_proj
    mid_stream = tok_float + gate_one * branch
    normed_two, inv_two = layer_norm(mid_stream)
    hidden_two = (normed_two * (1.0 + scale_two) + shift_two).astype(jnp.bfloat16)
    up_pre = contract("std,df->stf", hidden_two, up_full) + bias_up
    active = gelu_forward(up_pre).astype(jnp.bfloat16)
    mlp_out = contract("stf,fd->std", active, down_full) + bias_down
    block_out = ((mid_stream + gate_two * mlp_out) * slot_keep).astype(jnp.bfloat16)
    grad_out = cotangent.astype(jnp.float32) * slot_keep
    grad_gate_two = jnp.sum(grad_out * mlp_out, axis=1)
    grad_mlp = grad_out * gate_two
    grad_mlp_half = grad_mlp.astype(jnp.bfloat16)
    down_local = contract("stf,std->fd", active, grad_mlp_half)
    grad_up = contract("std,fd->stf", grad_mlp_half, down_full) * gelu_slope(up_pre)
    grad_up_half = grad_up.astype(jnp.bfloat16)
    up_local = contract("std,stf->df", hidden_two, grad_up_half)
    mlp_bias_local = jnp.concatenate(
        [
            jnp.zeros((2 * HW + D,), jnp.float32),
            jnp.sum(grad_up, axis=(0, 1)),
            jnp.sum(grad_mlp, axis=(0, 1)),
        ]
    )
    up_weight_grad, down_weight_grad, mlp_bias_grad = reduce_bucket(
        up_local, down_local, mlp_bias_local
    )
    grad_hidden_two = contract("stf,df->std", grad_up_half, up_full)
    grad_shift_two = jnp.sum(grad_hidden_two, axis=1)
    grad_scale_two = jnp.sum(grad_hidden_two * normed_two, axis=1)
    grad_mid = grad_out + norm_back(grad_hidden_two * (1.0 + scale_two), normed_two, inv_two)
    grad_gate_one = jnp.sum(grad_mid * branch, axis=1)
    grad_branch = grad_mid * gate_one
    grad_branch_half = grad_branch.astype(jnp.bfloat16)
    grad_attended = contract("std,ed->ste", grad_branch_half, proj_full).astype(jnp.bfloat16)
    proj_local = contract("ste,std->ed", attended, grad_branch_half)
    grad_heads = split_heads(grad_attended)
    out_heads = split_heads(attended)
    row_delta = jnp.transpose(
        jnp.sum(grad_heads.astype(jnp.float32) * out_heads.astype(jnp.float32), axis=-1), (0, 2, 1)
    )[..., None]
    scores_again = contract("sqhd,skhd->shqk", query_heads, key_heads) * scale_dot
    probs_float = jnp.exp(scores_again - log_total)
    grad_probs = contract("sqhd,skhd->shqk", grad_heads, value_heads)
    grad_scores = (probs_float * (grad_probs - row_delta) * scale_dot).astype(jnp.bfloat16)
    grad_query = contract("shqk,skhd->sqhd", grad_scores, key_heads).reshape(queries.shape)
    key_partial = contract("shqk,sqhd->skhd", grad_scores, query_heads).reshape(keys_all.shape)
    value_partial = contract(
        "shqk,sqhd->skhd", probs_float.astype(jnp.bfloat16), grad_heads
    ).reshape(values_all.shape)
    grad_key, grad_value = (
        lax.psum_scatter(
            key_partial.astype(jnp.bfloat16), "grp", scatter_dimension=1, tiled=True
        ).astype(jnp.float32),
        lax.psum_scatter(
            value_partial.astype(jnp.bfloat16), "grp", scatter_dimension=1, tiled=True
        ).astype(jnp.float32),
    )
    grad_qkv = jnp.concatenate([grad_query, grad_key, grad_value], axis=-1).astype(jnp.bfloat16)
    qkv_local = contract("std,ste->de", hidden_one, grad_qkv)
    attn_bias_local = jnp.concatenate(
        [
            jnp.sum(grad_query, axis=(0, 1)),
            jnp.sum(grad_value, axis=(0, 1)),
            jnp.sum(grad_branch, axis=(0, 1)),
            jnp.zeros((FF + D,), jnp.float32),
        ]
    )
    qkv_weight_grad, proj_weight_grad, attn_bias_grad = reduce_bucket(
        qkv_local, proj_local, attn_bias_local
    )
    main_bias_grad = mlp_bias_grad + attn_bias_grad
    grad_hidden_one = contract("ste,de->std", grad_qkv, qkv_full)
    grad_shift_one = jnp.sum(grad_hidden_one, axis=1)
    grad_scale_one = jnp.sum(grad_hidden_one * normed_one, axis=1)
    tokens_grad = (
        grad_mid + norm_back(grad_hidden_one * (1.0 + scale_one), normed_one, inv_one)
    ).astype(jnp.bfloat16)
    slot_mod_grad = jnp.concatenate(
        [
            grad_shift_one,
            grad_scale_one,
            grad_gate_one,
            grad_shift_two,
            grad_scale_two,
            grad_gate_two,
        ],
        axis=-1,
    )
    mod_local = jnp.dot(slot_pick.T, slot_mod_grad, precision=highest)
    mod_grad = lax.psum(mod_local, ("dp", "grp"))
    mod_grad_cols = lax.dynamic_slice_in_dim(
        mod_grad, lax.axis_index("grp") * col_width, col_width, 1
    )
    ada_weight_grad = jnp.dot(silu_cond.T, mod_grad_cols, precision=highest)
    ada_offset_grad = jnp.sum(mod_grad_cols, axis=0)
    cond_partial = jnp.dot(mod_grad_cols, ada_weight.T, precision=highest)
    cond_total = lax.psum(cond_partial, "grp")
    sigmoid_cond = jax.nn.sigmoid(condition)
    condition_grad = cond_total * sigmoid_cond * (1.0 + condition * (1.0 - sigmoid_cond))
    data_count = lax.axis_size("dp")
    square_sums = lax.psum(
        (
            jnp.sum(ada_weight_grad * ada_weight_grad),
            jnp.sum(ada_offset_grad * ada_offset_grad) / data_count,
            jnp.sum(qkv_weight_grad * qkv_weight_grad),
            jnp.sum(proj_weight_grad * proj_weight_grad),
            jnp.sum(up_weight_grad * up_weight_grad),
            jnp.sum(down_weight_grad * down_weight_grad),
            jnp.sum(main_bias_grad * main_bias_grad),
        ),
        ("dp", "grp"),
    )
    entry_counts = (D * 6 * D, 6 * D, D * 3 * HW, HW * D, D * FF, FF * D, 2 * HW + 2 * D + FF)
    results = []
    for index_param, (weight, first_mom, second_mom, gradient) in enumerate(
        (
            (ada_weight, ada_weight_mean, ada_weight_square, ada_weight_grad),
            (ada_offset, ada_offset_mean, ada_offset_square, ada_offset_grad),
            (qkv_weight, qkv_weight_mean, qkv_weight_square, qkv_weight_grad),
            (proj_weight, proj_weight_mean, proj_weight_square, proj_weight_grad),
            (up_weight, up_weight_mean, up_weight_square, up_weight_grad),
            (down_weight, down_weight_mean, down_weight_square, down_weight_grad),
            (main_bias, main_bias_mean, main_bias_square, main_bias_grad),
        )
    ):
        factor = clip_from(square_sums[index_param], entry_counts[index_param])
        weight_new, first_new, second_new = adam_update(
            weight, first_mom, second_mom, gradient, factor
        )
        results.append((gradient, weight_new, first_new, second_new))
    return (
        block_out,
        tokens_grad,
        condition_grad,
        results[0][0],
        results[0][1],
        results[0][2],
        results[0][3],
        results[1][0],
        results[1][1],
        results[1][2],
        results[1][3],
        results[2][0],
        results[2][1],
        results[2][2],
        results[2][3],
        results[3][0],
        results[3][1],
        results[3][2],
        results[3][3],
        results[4][0],
        results[4][1],
        results[4][2],
        results[4][3],
        results[5][0],
        results[5][1],
        results[5][2],
        results[5][3],
        results[6][0],
        results[6][1],
        results[6][2],
        results[6][3],
    )


def solution(mesh):
    return jax.shard_map(
        local,
        mesh=mesh,
        in_specs=(
            P("dp", "grp", None),
            P("dp", "grp", None),
            P(None, "dp"),
            P("dp"),
            P("dp"),
            P("dp", "grp"),
            P("dp", "grp"),
            P("dp", "grp"),
            P("grp"),
            P("grp"),
            P("grp"),
            P("dp", "grp"),
            P("dp", "grp"),
            P("dp", "grp"),
            P("dp", "grp"),
            P("dp", "grp"),
            P("dp", "grp"),
            P("dp", "grp"),
            P("dp", "grp"),
            P("dp", "grp"),
            P("dp", "grp"),
            P("dp", "grp"),
            P("dp", "grp"),
            P(("dp", "grp")),
            P(("dp", "grp")),
            P(("dp", "grp")),
        ),
        out_specs=(
            P("dp", "grp", None),
            P("dp", "grp", None),
            P(None, "dp"),
            P("dp", "grp"),
            P("dp", "grp"),
            P("dp", "grp"),
            P("dp", "grp"),
            P("grp"),
            P("grp"),
            P("grp"),
            P("grp"),
            P("dp", "grp"),
            P("dp", "grp"),
            P("dp", "grp"),
            P("dp", "grp"),
            P("dp", "grp"),
            P("dp", "grp"),
            P("dp", "grp"),
            P("dp", "grp"),
            P("dp", "grp"),
            P("dp", "grp"),
            P("dp", "grp"),
            P("dp", "grp"),
            P("dp", "grp"),
            P("dp", "grp"),
            P("dp", "grp"),
            P("dp", "grp"),
            P(("dp", "grp")),
            P(("dp", "grp")),
            P(("dp", "grp")),
            P(("dp", "grp")),
        ),
        check_vma=False,
    )
```

profile of v0, /device:TPU:0, one launch (start us, length us, event | category | flops | bytes accessed | tf_op | source)
XLA Modules:
  0.0 1611.9 jit_solution(4762603608129044166)
XLA Ops:
  21.1 80.3 %all-reduce.1 = bf16[9216]{0:T(1024)(128)(2,1)S(1)} all-reduce(bf16[9216]{0:T(1024)(128)(2,1)S(1)} %dynamic-update-slice.1), channel_id=1, replica_groups=mesh['dp'=16,'grp'=2] {'dp'}, use_global_device_ids=true, to_apply=%add.1 | all-reduce | flops 9216 | bytes 36864
  102.8 96.0 %all-reduce.11.cloned.1.call-done = f32[24,6912]{1,0:T(8,128)} async-done(((f32[24,6912]{1,0:T(8,128)}), f32[24,6912]{1,0:T(8,128)}) %all-reduce.11.cloned.1.call-update) | async-done | bytes 663568 | tf_op jit(solution)/shard_map/psum | solution.py:164
  258.9 49.0 %all-gather.16.cloned.1.call-done = bf16[1152,1152]{1,0:T(8,128)(2,1)} async-done(((bf16[72,1152]{1,0:T(8,128)(2,1)}), bf16[1152,1152]{1,0:T(8,128)(2,1)}) %all-gather.16.cloned.1.call-update) | async-done | bytes 2654224 | tf_op jit(solution)/shard_map/all_gather | solution.py:146
  315.3 128.1 %all-gather.18.cloned.1.call-done = bf16[1152,4608]{1,0:T(8,128)(2,1)} async-done(((bf16[72,4608]{1,0:T(8,128)(2,1)}), bf16[1152,4608]{1,0:T(8,128)(2,1)}) %all-gather.18.cloned.1.call-update) | async-done | bytes 10616848 | tf_op jit(solution)/shard_map/all_gather | solution.py:147
  443.4 13.2 fusion.10
  456.6 122.1 %all-gather.20.cloned.1.call-done = bf16[4608,1152]{1,0:T(8,128)(2,1)} async-done(((bf16[288,1152]{1,0:T(8,128)(2,1)}), bf16[4608,1152]{1,0:T(8,128)(2,1)}) %all-gather.20.cloned.1.call-update) | async-done | bytes 10616848 | tf_op jit(solution)/shard_map/all_gather | solution.py:148
  578.7 17.8 %fusion.96 = (bf16[4608]{0:T(1024)(128)(2,1)}, bf16[2,256,4608]{2,1,0:T(8,128)(2,1)}) fusion(f32[2,256,4608]{2,1,0:T(8,128)} %fusion.10, f32[4608]{0:T(1024)S(1)} %copy-done.45, bf16[4608,1152]{1,0:T(8,128)(2,1)} %all-gather.20.cloned.1.call-done, bf16[2,256,1152]{2,1,0:T(8,128)(2,1)} %param.27, f32[2]{0:T(128)S(1)} %copy-done.77, f32[2,1152]{1,0:T(2,128)S(1)} %copy-done.52), kind=kOutput, calls=%fused_computation.181 | convolution fusion | flops 5487717888 | bytes 25989128 | tf_op jit(solution)/shard_map/std,fd->stf/dot_general | solution.py:30
  596.5 12.3 multiply_reduce_fusion.2
  608.9 15.3 fusion.51
  630.1 8.5 convolution_convert_fusion.1
  644.6 9.6 multiply_convert_fusion
  677.1 9.5 fusion.2
  687.9 13.2 fusion.1
  712.9 76.1 %all-reduce.7 = (bf16[16,576]{1,0:T(8,128)(2,1)}, bf16[16,576]{1,0:T(8,128)(2,1)}) all-reduce(bf16[16,576]{1,0:T(8,128)(2,1)} %convert_element_type.197, bf16[16,576]{1,0:T(8,128)(2,1)} %convert_element_type.194), channel_id=14, replica_groups=mesh['dp'=16,'grp'=2] {'dp'}, use_global_device_ids=true, to_apply=%region_50.51.clone | all-reduce | flops 18432 | bytes 73728
  796.0 11.1 fusion
  808.7 10.5 fusion.44
  822.8 143.8 %reduce-scatter.47.cloned.1.call-done = bf16[72,3456]{1,0:T(8,128)(2,1)} async-done(((bf16[1152,3456]{1,0:T(8,128)(2,1)}), bf16[72,3456]{1,0:T(8,128)(2,1)}) %reduce-scatter.47.cloned.1.call-update) | async-done | bytes 497680
  968.9 184.4 %reduce-scatter.35.cloned.1.call-done = bf16[288,1152]{1,0:T(8,128)(2,1)} async-done(((bf16[4608,1152]{1,0:T(8,128)(2,1)}), bf16[288,1152]{1,0:T(8,128)(2,1)}) %reduce-scatter.35.cloned.1.call-update) | async-done | bytes 663568 | tf_op jit(solution)/shard_map/reduce_scatter | solution.py:85
  1163.9 10.6 reduce-scatter.43.cloned.1.call-done
  1176.1 188.4 %reduce-scatter.31.cloned.1.call-done = bf16[72,4608]{1,0:T(8,128)(2,1)} async-done(((bf16[1152,4608]{1,0:T(8,128)(2,1)}), bf16[72,4608]{1,0:T(8,128)(2,1)}) %reduce-scatter.31.cloned.1.call-update) | async-done | bytes 663568 | tf_op jit(solution)/shard_map/reduce_scatter | solution.py:82
  1364.5 132.0 %all-reduce.13.cloned.1.call-done = f32[24,6912]{1,0:T(8,128)} async-done(((f32[24,6912]{1,0:T(8,128)}), f32[24,6912]{1,0:T(8,128)}) %all-reduce.13.cloned.1.call-update) | async-done | bytes 663568 | tf_op jit(solution)/shard_map/psum | solution.py:288
  1509.8 10.6 reduce-scatter.37.cloned.1.call-done
  1522.3 10.4 reduce-scatter.41.cloned.1.call-done
  1546.9 41.3 %all-reduce.6 = (f32[]{:T(128)}, f32[]{:T(128)}, f32[]{:T(128)}, f32[]{:T(128)}, f32[]{:T(128)}, /*index=5*/f32[]{:T(128)}, f32[]{:T(128)}) all-reduce(f32[]{:T(128)} %get-tuple-element.109, f32[]{:T(128)S(6)} %div.173, f32[]{:T(128)} %get-tuple-element.79, f32[]{:T(128)} %get-tuple-element.77, ...), channel_id=1, replica_groups=mesh['dp'=16,'grp'=2] {'dp','grp'}, use_global_device_ids=true, to_apply=%region_23.24 | all-reduce | flops 7 | bytes 56 | tf_op jit(solution)/shard_map/psum | solution.py:299
  (315 shorter events, 194.2 us)
Async XLA Ops:
  8.0 190.7 %all-reduce.11.cloned.1.call-start = ((), (), s32[]{:S(2)}) async-start(), calls=%async_computation.12 | async-start | bytes 1327104 | tf_op jit(solution)/shard_map/psum | solution.py:164
  11.6 189.2 %all-gather.10.cloned.1.call-start = ((), (), s32[]{:S(2)}) async-start(), calls=%async_computation.13 | async-start | bytes 8460288 | tf_op jit(solution)/shard_map/all_gather | solution.py:145
  15.6 213.6 %all-gather.12.cloned.1.call-start = ((), (), s32[]{:S(2)}) async-start(), calls=%async_computation.14 | async-start | bytes 3538944 | tf_op jit(solution)/shard_map/all_gather | solution.py:185
  211.9 27.0 %all-gather.14.cloned.1.call-start = ((), (), s32[]{:S(2)}) async-start(), calls=%async_computation.15 | async-start | bytes 3538944 | tf_op jit(solution)/shard_map/all_gather | solution.py:184
  214.8 93.0 %all-gather.16.cloned.1.call-start = ((), (), s32[]{:S(2)}) async-start(), calls=%async_computation.16 | async-start | bytes 2820096 | tf_op jit(solution)/shard_map/all_gather | solution.py:146
  218.0 225.3 %all-gather.18.cloned.1.call-start = ((), (), s32[]{:S(2)}) async-start(), calls=%async_computation.17 | async-start | bytes 11280384 | tf_op jit(solution)/shard_map/all_gather | solution.py:147
  221.7 357.0 %all-gather.20.cloned.1.call-start = ((), (), s32[]{:S(2)}) async-start(), calls=%async_computation.18 | async-start | bytes 11280384 | tf_op jit(solution)/shard_map/all_gather | solution.py:148
  226.3 450.4 %reduce-scatter.29.cloned.1.call-start = ((), (), s32[]{:S(2)}) async-start(), calls=%async_computation.20 | async-start | bytes 3538944 | tf_op jit(solution)/shard_map/reduce_scatter | solution.py:252
  642.9 33.9 %reduce-scatter.27.cloned.1.call-start = ((), (), s32[]{:S(2)}) async-start(), calls=%async_computation.19 | async-start | bytes 3538944 | tf_op jit(solution)/shard_map/reduce_scatter | solution.py:249
  660.5 160.4 %reduce-scatter.49.cloned.1.call-start = ((), (), s32[]{:S(2)}) async-start(), calls=%async_computation.31 | async-start | bytes 2820096
  666.6 300.0 %reduce-scatter.47.cloned.1.call-start = ((), (), s32[]{:S(2)}) async-start(), calls=%async_computation.30 | async-start | bytes 8460288
  686.7 466.6 %reduce-scatter.35.cloned.1.call-start = ((), (), s32[]{:S(2)}) async-start(), calls=%async_computation.24 | async-start | bytes 11280384 | tf_op jit(solution)/shard_map/reduce_scatter | solution.py:85
  701.1 461.8 %reduce-scatter.45.cloned.1.call-start = ((), (), s32[]{:S(2)}) async-start(), calls=%async_computation.29 | async-start | bytes 221184
  792.4 382.1 %reduce-scatter.43.cloned.1.call-start = ((), (), s32[]{:S(2)}) async-start(), calls=%async_computation.28 | async-start | bytes 221184
  796.0 568.6 %reduce-scatter.31.cloned.1.call-start = ((), (), s32[]{:S(2)}) async-start(), calls=%async_computation.22 | async-start | bytes 11280384 | tf_op jit(solution)/shard_map/reduce_scatter | solution.py:82
  807.1 689.4 %all-reduce.13.cloned.1.call-start = ((), (), s32[]{:S(2)}) async-start(), calls=%async_computation.21 | async-start | bytes 1327104 | tf_op jit(solution)/shard_map/psum | solution.py:288
  820.8 687.2 %reduce-scatter.39.cloned.1.call-start = ((), (), s32[]{:S(2)}) async-start(), calls=%async_computation.26 | async-start | bytes 442368
  822.7 333.0 %copy-start.64 = (f32[2,256]{1,0:T(2,128)S(1)}, f32[2,256]{1,0:T(2,128)}, u32[]{:S(2)}) copy-start(f32[2,256]{1,0:T(2,128)} %copy-done.63) | copy-start | bytes 6148
  822.8 697.6 %reduce-scatter.37.cloned.1.call-start = ((), (), s32[]{:S(2)}) async-start(), calls=%async_computation.25 | async-start | bytes 1327104
  968.9 563.8 %reduce-scatter.41.cloned.1.call-start = ((), (), s32[]{:S(2)}) async-start(), calls=%async_computation.27 | async-start | bytes 1327104
  1155.6 388.7 %reduce-scatter.33.cloned.1.call-start = ((), (), s32[]{:S(2)}) async-start(), calls=%async_computation.23 | async-start | bytes 995328 | tf_op jit(solution)/shard_map/reduce_scatter | solution.py:93
  1155.7 340.8 %copy-start.9 = (f32[72,3456]{1,0:T(8,128)S(1)}, f32[72,3456]{1,0:T(8,128)}, u32[]{:S(2)}) copy-start(f32[72,3456]{1,0:T(8,128)} %param.31) | copy-start | bytes 2985988
  1160.1 344.2 %copy-start.41 = (f32[24,72]{1,0:T(8,128)S(1)}, f32[24,72]{1,0:T(8,128)}, u32[]{:S(2)}) copy-start(f32[24,72]{1,0:T(8,128)} %param.28) | copy-start | bytes 20740
  1175.5 418.2 %copy-start.47 = (f32[288]{0:T(512)}, f32[288]{0:T(512)S(1)}, u32[]{:S(2)}) copy-start(f32[288]{0:T(512)S(1)} %add_reduce_fusion) | copy-start | bytes 3460
  (75 other events, 3561.1 us)
Sparse Core Ops, SparseCore 0:
  14.7 184.0 all-reduce.10
  212.0 12.2 all-gather.11
  226.5 12.3 all-gather.13
  242.4 65.4 all-gather.15
  310.9 132.4 all-gather.17
  446.9 131.6 all-gather.19
  643.1 8.0 reduce-scatter.28
  660.6 8.2 reduce-scatter.26
  674.8 125.1 reduce-scatter.48
  806.7 159.8 reduce-scatter.46
  972.4 180.8 reduce-scatter.34
  1156.0 6.8 reduce-scatter.44
  1165.8 8.6 reduce-scatter.42
  1181.2 183.2 reduce-scatter.30
  1370.2 126.3 all-reduce.12
  1499.3 8.6 reduce-scatter.38
  1510.8 9.4 reduce-scatter.36
  1523.2 9.4 reduce-scatter.40
  1535.0 9.2 reduce-scatter.32
Sparse Core Ops, SparseCore 1:
  15.8 113.6 all-gather.9
where the time goes:
time: 1620 us; the launch traced here: 1610 us
  waiting for transfers between devices  1090 us (67%)
  blocking collectives  213 us (13%)
  matrix products  172 us (11%)
  local copies, waits for them, and re-layouts  65.2 us (4%)
  other arithmetic  42.9 us (3%)
  between operations  23.7 us (1%)
    reduce_scatter x1, waiting for transfers between devices, reduce_bucket(): lax.psum_scatter(first_grad.astype(jnp.bfloat16), 'dp', scatter_dimension...  188 us
    reduce_scatter x1, waiting for transfers between devices, reduce_bucket(): lax.psum_scatter(second_grad.astype(jnp.bfloat16), 'dp', scatter_dimensio...  184 us
    unnamed x27, waiting for transfers between devices  179 us
    dot_general x18, matrix products, contract(): return jnp.einsum(pattern, left, right, preferred_element_type=jnp.float32)  163 us
    unnamed x3, blocking collectives  159 us
    psum x1, waiting for transfers between devices, local(): mod_grad = lax.psum(mod_local, ('dp', 'grp'))  132 us
    all_gather x1, waiting for transfers between devices, local(): lax.all_gather(up_part, 'dp', axis=0, tiled=True)  128 us
    all_gather x1, waiting for transfers between devices, local(): lax.all_gather(down_part, 'dp', axis=0, tiled=True)  122 us
  transfers between devices with their start and end apart: 20, of which 15 were waited for; matrix products, arithmetic and copies ran while one was open for 11% of the time, Pallas kernels for 0%

commit v1 on v0

--- a/solution.py
+++ b/solution.py
@@ -76,31 +76,82 @@
     return values.reshape(values.shape[:-1] + (HEADS, HD))
 
 
-def reduce_bucket(first_grad, second_grad, bias_grad):
-    bias_rows = bias_grad.reshape(lax.axis_size("dp"), -1)
-    summed = (
-        lax.psum_scatter(
-            first_grad.astype(jnp.bfloat16), "dp", scatter_dimension=0, tiled=True
-        ).astype(jnp.float32),
-        lax.psum_scatter(
-            second_grad.astype(jnp.bfloat16), "dp", scatter_dimension=0, tiled=True
-        ).astype(jnp.float32),
-        lax.psum_scatter(
-            bias_rows.astype(jnp.bfloat16), "dp", scatter_dimension=0, tiled=True
-        ).astype(jnp.float32),
-    )
-    owned = (
-        lax.psum_scatter(
-            summed[0].astype(jnp.bfloat16), "grp", scatter_dimension=1, tiled=True
-        ).astype(jnp.float32),
-        lax.psum_scatter(
-            summed[1].astype(jnp.bfloat16), "grp", scatter_dimension=1, tiled=True
-        ).astype(jnp.float32),
-        lax.psum_scatter(
-            summed[2].astype(jnp.bfloat16), "grp", scatter_dimension=1, tiled=True
-        ).astype(jnp.float32),
-    )
-    return (owned[0], owned[1], owned[2].reshape(-1))
+def swap(values):
+    return lax.ppermute(values, "grp", [(0, 1), (1, 0)])
+
+
+ACROSS = (3, 2, 0, 1)
+ALONG = (3, 2, 1, 0)
+
+
+def data_bit(bit):
+    return lax.rem(lax.axis_index("dp") // 2**bit, 2) == 1
+
+
+def trade(values, bit):
+    size = lax.axis_size("dp")
+    return lax.ppermute(values, "dp", [(at, at ^ 2**bit) for at in range(size)])
+
+
+def gather_data(values, order):
+    shape = values.shape
+    held = []
+    for bit in order:
+        other = trade(values, bit)
+        upper = data_bit(bit)
+        place = sum(have > bit for have in held)
+        values = jnp.stack(
+            [jnp.where(upper, other, values), jnp.where(upper, values, other)], axis=place
+        )
+        held.append(bit)
+    return values.reshape((-1,) + shape[1:])
+
+
+def scatter_data(values, order, wire):
+    rows = values.shape[0] // lax.axis_size("dp")
+    left = sorted(order, reverse=True)
+    shape = (rows,) + values.shape[1:]
+    values = values.reshape((2,) * len(left) + shape)
+    for bit in reversed(order):
+        place = left.index(bit)
+        low = lax.index_in_dim(values, 0, place, keepdims=False)
+        high = lax.index_in_dim(values, 1, place, keepdims=False)
+        upper = data_bit(bit)
+        kept = jnp.where(upper, high, low)
+        sent = jnp.where(upper, low, high).astype(wire)
+        values = kept + trade(sent, bit).astype(jnp.float32)
+        left.remove(bit)
+    return values
+
+
+def total_over_all(values):
+    for bit in ALONG:
+        values = values + trade(values, bit)
+    return values + swap(values)
+
+
+def natural(own, other):
+    first = lax.axis_index("grp") == 0
+    return jnp.concatenate(
+        [jnp.where(first, own, other), jnp.where(first, other, own)], axis=-1
+    )
+
+
+def cut(values):
+    half = values.shape[-1] // 2
+    first = lax.axis_index("grp") == 0
+    low, high = values[..., :half], values[..., half:]
+    return jnp.where(first, low, high), jnp.where(first, high, low)
+
+
+def weight_halves(weight, order):
+    own = gather_data(weight.astype(jnp.bfloat16), order)
+    return own, swap(own)
+
+
+def weight_grad(own, other, order):
+    arrived = swap(other.astype(jnp.bfloat16))
+    return scatter_data(own + arrived.astype(jnp.float32), order, jnp.bfloat16)
 
 
 def local(
@@ -134,38 +185,34 @@
     latents = condition.shape[0]
     slot_count = tokens.shape[0]
     scale_dot = 1.0 / math.sqrt(HD)
-    qkv_part, proj_part, up_part, down_part, bias_part = (
-        lax.all_gather(qkv_weight.astype(jnp.bfloat16), "grp", axis=1, tiled=True),
-        lax.all_gather(proj_weight.astype(jnp.bfloat16), "grp", axis=1, tiled=True),
-        lax.all_gather(up_weight.astype(jnp.bfloat16), "grp", axis=1, tiled=True),
-        lax.all_gather(down_weight.astype(jnp.bfloat16), "grp", axis=1, tiled=True),
-        lax.all_gather(main_bias.astype(jnp.bfloat16), "grp", axis=0, tiled=True),
-    )
-    qkv_full, proj_full, up_full, down_full, bias_full = (
-        lax.all_gather(qkv_part, "dp", axis=0, tiled=True),
-        lax.all_gather(proj_part, "dp", axis=0, tiled=True),
-        lax.all_gather(up_part, "dp", axis=0, tiled=True),
-        lax.all_gather(down_part, "dp", axis=0, tiled=True),
-        lax.all_gather(bias_part, "dp", axis=0, tiled=True),
-    )
-    bias_float = bias_full.astype(jnp.float32)
+    data_count = lax.axis_size("dp")
+    data_at = lax.axis_index("dp")
+    bias_share = main_bias.shape[0]
+    packed = jnp.concatenate(
+        [main_bias.astype(jnp.bfloat16).astype(jnp.float32), latent_of.astype(jnp.float32)]
+    )
+    packed_all = gather_data(packed[None], ALONG)
+    packed_other = swap(packed_all)
+    slots_named = packed_all[:, bias_share:].reshape(-1).astype(jnp.int32)
+    bias_float = natural(packed_all[:, :bias_share], packed_other[:, :bias_share]).reshape(-1)
     bias_query = bias_float[:HW]
     bias_value = bias_float[HW : 2 * HW]
     bias_proj = bias_float[2 * HW : 2 * HW + D]
     bias_up = bias_float[2 * HW + D : 2 * HW + D + FF]
     bias_down = bias_float[2 * HW + D + FF :]
     silu_cond = jax.nn.silu(condition)
-    col_width = ada_weight.shape[1]
-    first_data = jnp.where(lax.axis_index("dp") == 0, 1.0, 0.0).astype(jnp.float32)
+    first_data = jnp.where(data_at == 0, 1.0, 0.0).astype(jnp.float32)
     mod_piece = jnp.dot(silu_cond, ada_weight, precision=highest) + first_data * ada_offset
-    mod_spread = lax.dynamic_update_slice_in_dim(
-        jnp.zeros((latents, 6 * D), jnp.float32), mod_piece, lax.axis_index("grp") * col_width, 1
-    )
-    mod_table = lax.psum(mod_spread, ("dp", "grp"))
-    slot_pick = (latent_of[:, None] == jnp.arange(latents, dtype=jnp.int32)[None, :]).astype(
+    all_pick = (slots_named[:, None] == jnp.arange(latents, dtype=jnp.int32)[None, :]).astype(
         jnp.float32
     )
-    slot_mod = jnp.dot(slot_pick, mod_table, precision=highest)[:, None, :]
+    slot_piece = jnp.dot(all_pick, mod_piece, precision=highest)
+    mod_own = scatter_data(slot_piece, ALONG, jnp.float32)
+    slot_mod = natural(mod_own, swap(mod_own))[:, None, :]
+    qkv_own, qkv_other = weight_halves(qkv_weight, ALONG)
+    proj_own, proj_other = weight_halves(proj_weight, ACROSS)
+    up_own, up_other = weight_halves(up_weight, ACROSS)
+    down_own, down_other = weight_halves(down_weight, ALONG)
     shift_one = slot_mod[..., :D]
     scale_one = slot_mod[..., D : 2 * D]
     gate_one = slot_mod[..., 2 * D : 3 * D]
@@ -176,14 +223,15 @@
     tok_float = tokens.astype(jnp.float32)
     normed_one, inv_one = layer_norm(tok_float)
     hidden_one = (normed_one * (1.0 + scale_one) + shift_one).astype(jnp.bfloat16)
-    projected = contract("std,de->ste", hidden_one, qkv_full)
+    projected = natural(
+        contract("std,de->ste", hidden_one, qkv_own), contract("std,de->ste", hidden_one, qkv_other)
+    )
     queries = (projected[..., :HW] + bias_query).astype(jnp.bfloat16)
     keys_own = projected[..., HW : 2 * HW].astype(jnp.bfloat16)
     values_own = (projected[..., 2 * HW :] + bias_value).astype(jnp.bfloat16)
-    keys_all, values_all = (
-        lax.all_gather(keys_own, "grp", axis=1, tiled=True),
-        lax.all_gather(values_own, "grp", axis=1, tiled=True),
-    )
+    own_tokens = keys_own.shape[1]
+    keys_all = jnp.concatenate([keys_own, swap(keys_own)], axis=1)
+    values_all = jnp.concatenate([values_own, swap(values_own)], axis=1)
     query_heads = split_heads(queries)
     key_heads = split_heads(keys_all)
     value_heads = split_heads(values_all)
@@ -196,41 +244,69 @@
         .astype(jnp.bfloat16)
         .reshape(queries.shape)
     )
-    branch = contract("ste,ed->std", attended, proj_full) + bias_proj
+    branch = (
+        natural(
+            contract("ste,ed->std", attended, proj_own),
+            contract("ste,ed->std", attended, proj_other),
+        )
+        + bias_proj
+    )
     mid_stream = tok_float + gate_one * branch
     normed_two, inv_two = layer_norm(mid_stream)
     hidden_two = (normed_two * (1.0 + scale_two) + shift_two).astype(jnp.bfloat16)
-    up_pre = contract("std,df->stf", hidden_two, up_full) + bias_up
+    up_pre = (
+        natural(
+            contract("std,df->stf", hidden_two, up_own),
+            contract("std,df->stf", hidden_two, up_other),
+        )
+        + bias_up
+    )
     active = gelu_forward(up_pre).astype(jnp.bfloat16)
-    mlp_out = contract("stf,fd->std", active, down_full) + bias_down
+    mlp_out = (
+        natural(
+            contract("stf,fd->std", active, down_own), contract("stf,fd->std", active, down_other)
+        )
+        + bias_down
+    )
     block_out = ((mid_stream + gate_two * mlp_out) * slot_keep).astype(jnp.bfloat16)
     grad_out = cotangent.astype(jnp.float32) * slot_keep
     grad_gate_two = jnp.sum(grad_out * mlp_out, axis=1)
     grad_mlp = grad_out * gate_two
     grad_mlp_half = grad_mlp.astype(jnp.bfloat16)
-    down_local = contract("stf,std->fd", active, grad_mlp_half)
-    grad_up = contract("std,fd->stf", grad_mlp_half, down_full) * gelu_slope(up_pre)
+    mlp_own, mlp_other = cut(grad_mlp_half)
+    down_weight_grad = weight_grad(
+        contract("stf,std->fd", active, mlp_own),
+        contract("stf,std->fd", active, mlp_other),
+        ALONG,
+    )
+    grad_up = (
+        contract("std,fd->stf", mlp_own, down_own) + contract("std,fd->stf", mlp_other, down_other)
+    ) * gelu_slope(up_pre)
     grad_up_half = grad_up.astype(jnp.bfloat16)
-    up_local = contract("std,stf->df", hidden_two, grad_up_half)
-    mlp_bias_local = jnp.concatenate(
-        [
-            jnp.zeros((2 * HW + D,), jnp.float32),
-            jnp.sum(grad_up, axis=(0, 1)),
-            jnp.sum(grad_mlp, axis=(0, 1)),
-        ]
-    )
-    up_weight_grad, down_weight_grad, mlp_bias_grad = reduce_bucket(
-        up_local, down_local, mlp_bias_local
-    )
-    grad_hidden_two = contract("stf,df->std", grad_up_half, up_full)
+    rise_own, rise_other = cut(grad_up_half)
+    up_weight_grad = weight_grad(
+        contract("std,stf->df", hidden_two, rise_own),
+        contract("std,stf->df", hidden_two, rise_other),
+        ACROSS,
+    )
+    grad_hidden_two = contract("stf,df->std", rise_own, up_own) + contract(
+        "stf,df->std", rise_other, up_other
+    )
     grad_shift_two = jnp.sum(grad_hidden_two, axis=1)
     grad_scale_two = jnp.sum(grad_hidden_two * normed_two, axis=1)
     grad_mid = grad_out + norm_back(grad_hidden_two * (1.0 + scale_two), normed_two, inv_two)
     grad_gate_one = jnp.sum(grad_mid * branch, axis=1)
     grad_branch = grad_mid * gate_one
     grad_branch_half = grad_branch.astype(jnp.bfloat16)
-    grad_attended = contract("std,ed->ste", grad_branch_half, proj_full).astype(jnp.bfloat16)
-    proj_local = contract("ste,std->ed", attended, grad_branch_half)
+    fork_own, fork_other = cut(grad_branch_half)
+    grad_attended = (
+        contract("std,ed->ste", fork_own, proj_own) + contract("std,ed->ste", fork_other, proj_other)
+    ).astype(jnp.bfloat16)
+    proj_weight_grad = weight_grad(
+        contract("ste,std->ed", attended, fork_own),
+        contract("ste,std->ed", attended, fork_other),
+        ACROSS,
+    )
     grad_heads = split_heads(grad_attended)
     out_heads = split_heads(attended)
     row_delta = jnp.transpose(
@@ -245,29 +321,31 @@
     value_partial = contract(
         "shqk,sqhd->skhd", probs_float.astype(jnp.bfloat16), grad_heads
     ).reshape(values_all.shape)
-    grad_key, grad_value = (
-        lax.psum_scatter(
-            key_partial.astype(jnp.bfloat16), "grp", scatter_dimension=1, tiled=True
-        ).astype(jnp.float32),
-        lax.psum_scatter(
-            value_partial.astype(jnp.bfloat16), "grp", scatter_dimension=1, tiled=True
-        ).astype(jnp.float32),
-    )
+    grad_key = key_partial[:, :own_tokens] + swap(
+        key_partial[:, own_tokens:].astype(jnp.bfloat16)
+    ).astype(jnp.float32)
+    grad_value = value_partial[:, :own_tokens] + swap(
+        value_partial[:, own_tokens:].astype(jnp.bfloat16)
+    ).astype(jnp.float32)
     grad_qkv = jnp.concatenate([grad_query, grad_key, grad_value], axis=-1).astype(jnp.bfloat16)
-    qkv_local = contract("std,ste->de", hidden_one, grad_qkv)
-    attn_bias_local = jnp.concatenate(
+    trio_own, trio_other = cut(grad_qkv)
+    qkv_weight_grad = weight_grad(
+        contract("std,ste->de", hidden_one, trio_own),
+        contract("std,ste->de", hidden_one, trio_other),
+        ALONG,
+    )
+    bias_local = jnp.concatenate(
         [
             jnp.sum(grad_query, axis=(0, 1)),
             jnp.sum(grad_value, axis=(0, 1)),
             jnp.sum(grad_branch, axis=(0, 1)),
-            jnp.zeros((FF + D,), jnp.float32),
+            jnp.sum(grad_up, axis=(0, 1)),
+            jnp.sum(grad_mlp, axis=(0, 1)),
         ]
-    )
-    qkv_weight_grad, proj_weight_grad, attn_bias_grad = reduce_bucket(
-        qkv_local, proj_local, attn_bias_local
-    )
-    main_bias_grad = mlp_bias_grad + attn_bias_grad
-    grad_hidden_one = contract("ste,de->std", grad_qkv, qkv_full)
+    ).reshape(data_count, -1)
+    grad_hidden_one = contract("ste,de->std", trio_own, qkv_own) + contract(
+        "ste,de->std", trio_other, qkv_other
+    )
     grad_shift_one = jnp.sum(grad_hidden_one, axis=1)
     grad_scale_one = jnp.sum(grad_hidden_one * normed_one, axis=1)
     tokens_grad = (
@@ -284,29 +362,38 @@
         ],
         axis=-1,
     )
-    mod_local = jnp.dot(slot_pick.T, slot_mod_grad, precision=highest)
-    mod_grad = lax.psum(mod_local, ("dp", "grp"))
-    mod_grad_cols = lax.dynamic_slice_in_dim(
-        mod_grad, lax.axis_index("grp") * col_width, col_width, 1
-    )
+    bias_own, bias_other = cut(bias_local)
+    mod_grad_own, mod_grad_other = cut(slot_mod_grad)
+    bias_entries = bias_own.size
+    vector_own = jnp.concatenate([bias_own.reshape(-1), mod_grad_own.reshape(-1)])
+    vector_other = jnp.concatenate([bias_other.reshape(-1), mod_grad_other.reshape(-1)])
+    vectors = gather_data((vector_own + swap(vector_other))[None], ALONG)
+    main_bias_grad = jnp.sum(
+        lax.dynamic_slice_in_dim(
+            vectors[:, :bias_entries].reshape(data_count, data_count, -1), data_at, 1, 1
+        ),
+        axis=(0, 1),
+    )
+    slot_rows = vectors[:, bias_entries:].reshape(data_count * slot_count, -1)
+    mod_grad_cols = jnp.dot(all_pick.T, slot_rows, precision=highest)
     ada_weight_grad = jnp.dot(silu_cond.T, mod_grad_cols, precision=highest)
     ada_offset_grad = jnp.sum(mod_grad_cols, axis=0)
     cond_partial = jnp.dot(mod_grad_cols, ada_weight.T, precision=highest)
-    cond_total = lax.psum(cond_partial, "grp")
+    cond_total = cond_partial + swap(cond_partial)
     sigmoid_cond = jax.nn.sigmoid(condition)
     condition_grad = cond_total * sigmoid_cond * (1.0 + condition * (1.0 - sigmoid_cond))
-    data_count = lax.axis_size("dp")
-    square_sums = lax.psum(
-        (
-            jnp.sum(ada_weight_grad * ada_weight_grad),
-            jnp.sum(ada_offset_grad * ada_offset_grad) / data_count,
-            jnp.sum(qkv_weight_grad * qkv_weight_grad),
-            jnp.sum(proj_weight_grad * proj_weight_grad),
-            jnp.sum(up_weight_grad * up_weight_grad),
-            jnp.sum(down_weight_grad * down_weight_grad),
-            jnp.sum(main_bias_grad * main_bias_grad),
-        ),
-        ("dp", "grp"),
+    square_sums = total_over_all(
+        jnp.stack(
+            [
+                jnp.sum(ada_weight_grad * ada_weight_grad),
+                jnp.sum(ada_offset_grad * ada_offset_grad) / data_count,
+                jnp.sum(qkv_weight_grad * qkv_weight_grad),
+                jnp.sum(proj_weight_grad * proj_weight_grad),
+                jnp.sum(up_weight_grad * up_weight_grad),
+                jnp.sum(down_weight_grad * down_weight_grad),
+                jnp.sum(main_bias_grad * main_bias_grad),
+            ]
+        )
     )
     entry_counts = (D * 6 * D, 6 * D, D * 3 * HW, HW * D, D * FF, FF * D, 2 * HW + 2 * D + FF)
     results = []
@@ -361,9 +448,295 @@
     )
 
 
+def reduce_bucket(first_grad, second_grad, bias_grad):
+    bias_rows = bias_grad.reshape(lax.axis_size("dp"), -1)
+    summed = (
+        lax.psum_scatter(
+            first_grad.astype(jnp.bfloat16), "dp", scatter_dimension=0, tiled=True
+        ).astype(jnp.float32),
+        lax.psum_scatter(
+            second_grad.astype(jnp.bfloat16), "dp", scatter_dimension=0, tiled=True
+        ).astype(jnp.float32),
+        lax.psum_scatter(
+            bias_rows.astype(jnp.bfloat16), "dp", scatter_dimension=0, tiled=True
+        ).astype(jnp.float32),
+    )
+    owned = (
+        lax.psum_scatter(
+            summed[0].astype(jnp.bfloat16), "grp", scatter_dimension=1, tiled=True
+        ).astype(jnp.float32),
+        lax.psum_scatter(
+            summed[1].astype(jnp.bfloat16), "grp", scatter_dimension=1, tiled=True
+        ).astype(jnp.float32),
+        lax.psum_scatter(
+            summed[2].astype(jnp.bfloat16), "grp", scatter_dimension=1, tiled=True
+        ).astype(jnp.float32),
+    )
+    return (owned[0], owned[1], owned[2].reshape(-1))
+
+
+def local_general(
+    tokens,
+    cotangent,
+    condition,
+    latent_of,
+    slot_valid,
+    ada_weight,
+    ada_weight_mean,
+    ada_weight_square,
+    ada_offset,
+    ada_offset_mean,
+    ada_offset_square,
+    qkv_weight,
+    qkv_weight_mean,
+    qkv_weight_square,
+    proj_weight,
+    proj_weight_mean,
+    proj_weight_square,
+    up_weight,
+    up_weight_mean,
+    up_weight_square,
+    down_weight,
+    down_weight_mean,
+    down_weight_square,
+    main_bias,
+    main_bias_mean,
+    main_bias_square,
+):
+    latents = condition.shape[0]
+    slot_count = tokens.shape[0]
+    scale_dot = 1.0 / math.sqrt(HD)
+    qkv_part, proj_part, up_part, down_part, bias_part = (
+        lax.all_gather(qkv_weight.astype(jnp.bfloat16), "grp", axis=1, tiled=True),
+        lax.all_gather(proj_weight.astype(jnp.bfloat16), "grp", axis=1, tiled=True),
+        lax.all_gather(up_weight.astype(jnp.bfloat16), "grp", axis=1, tiled=True),
+        lax.all_gather(down_weight.astype(jnp.bfloat16), "grp", axis=1, tiled=True),
+        lax.all_gather(main_bias.astype(jnp.bfloat16), "grp", axis=0, tiled=True),
+    )
+    qkv_full, proj_full, up_full, down_full, bias_full = (
+        lax.all_gather(qkv_part, "dp", axis=0, tiled=True),
+        lax.all_gather(proj_part, "dp", axis=0, tiled=True),
+        lax.all_gather(up_part, "dp", axis=0, tiled=True),
+        lax.all_gather(down_part, "dp", axis=0, tiled=True),
+        lax.all_gather(bias_part, "dp", axis=0, tiled=True),
+    )
+    bias_float = bias_full.astype(jnp.float32)
+    bias_query = bias_float[:HW]
+    bias_value = bias_float[HW : 2 * HW]
+    bias_proj = bias_float[2 * HW : 2 * HW + D]
+    bias_up = bias_float[2 * HW + D : 2 * HW + D + FF]
+    bias_down = bias_float[2 * HW + D + FF :]
+    silu_cond = jax.nn.silu(condition)
+    col_width = ada_weight.shape[1]
+    first_data = jnp.where(lax.axis_index("dp") == 0, 1.0, 0.0).astype(jnp.float32)
+    mod_piece = jnp.dot(silu_cond, ada_weight, precision=highest) + first_data * ada_offset
+    mod_spread = lax.dynamic_update_slice_in_dim(
+        jnp.zeros((latents, 6 * D), jnp.float32), mod_piece, lax.axis_index("grp") * col_width, 1
+    )
+    mod_table = lax.psum(mod_spread, ("dp", "grp"))
+    slot_pick = (latent_of[:, None] == jnp.arange(latents, dtype=jnp.int32)[None, :]).astype(
+        jnp.float32
+    )
+    slot_mod = jnp.dot(slot_pick, mod_table, precision=highest)[:, None, :]
+    shift_one = slot_mod[..., :D]
+    scale_one = slot_mod[..., D : 2 * D]
+    gate_one = slot_mod[..., 2 * D : 3 * D]
+    shift_two = slot_mod[..., 3 * D : 4 * D]
+    scale_two = slot_mod[..., 4 * D : 5 * D]
+    gate_two = slot_mod[..., 5 * D :]
+    slot_keep = slot_valid.astype(jnp.float32)[:, None, None]
+    tok_float = tokens.astype(jnp.float32)
+    normed_one, inv_one = layer_norm(tok_float)
+    hidden_one = (normed_one * (1.0 + scale_one) + shift_one).astype(jnp.bfloat16)
+    projected = contract("std,de->ste", hidden_one, qkv_full)
+    queries = (projected[..., :HW] + bias_query).astype(jnp.bfloat16)
+    keys_own = projected[..., HW : 2 * HW].astype(jnp.bfloat16)
+    values_own = (projected[..., 2 * HW :] + bias_value).astype(jnp.bfloat16)
+    keys_all, values_all = (
+        lax.all_gather(keys_own, "grp", axis=1, tiled=True),
+        lax.all_gather(values_own, "grp", axis=1, tiled=True),
+    )
+    query_heads = split_heads(queries)
+    key_heads = split_heads(keys_all)
+    value_heads = split_heads(values_all)
+    scores = contract("sqhd,skhd->shqk", query_heads, key_heads) * scale_dot
+    row_max = jnp.max(scores, axis=-1, keepdims=True)
+    log_total = row_max + jnp.log(jnp.sum(jnp.exp(scores - row_max), axis=-1, keepdims=True))
+    probs_half = jnp.exp(scores - log_total).astype(jnp.bfloat16)
+    attended = (
+        contract("shqk,skhd->sqhd", probs_half, value_heads)
+        .astype(jnp.bfloat16)
+        .reshape(queries.shape)
+    )
+    branch = contract("ste,ed->std", attended, proj_full) + bias_proj
+    mid_stream = tok_float + gate_one * branch
+    normed_two, inv_two = layer_norm(mid_stream)
+    hidden_two = (normed_two * (1.0 + scale_two) + shift_two).astype(jnp.bfloat16)
+    up_pre = contract("std,df->stf", hidden_two, up_full) + bias_up
+    active = gelu_forward(up_pre).astype(jnp.bfloat16)
+    mlp_out = contract("stf,fd->std", active, down_full) + bias_down
+    block_out = ((mid_stream + gate_two * mlp_out) * slot_keep).astype(jnp.bfloat16)
+    grad_out = cotangent.astype(jnp.float32) * slot_keep
+    grad_gate_two = jnp.sum(grad_out * mlp_out, axis=1)
+    grad_mlp = grad_out * gate_two
+    grad_mlp_half = grad_mlp.astype(jnp.bfloat16)
+    down_local = contract("stf,std->fd", active, grad_mlp_half)
+    grad_up = contract("std,fd->stf", grad_mlp_half, down_full) * gelu_slope(up_pre)
+    grad_up_half = grad_up.astype(jnp.bfloat16)
+    up_local = contract("std,stf->df", hidden_two, grad_up_half)
+    mlp_bias_local = jnp.concatenate(
+        [
+            jnp.zeros((2 * HW + D,), jnp.float32),
+            jnp.sum(grad_up, axis=(0, 1)),
+            jnp.sum(grad_mlp, axis=(0, 1)),
+        ]
+    )
+    up_weight_grad, down_weight_grad, mlp_bias_grad = reduce_bucket(
+        up_local, down_local, mlp_bias_local
+    )
+    grad_hidden_two = contract("stf,df->std", grad_up_half, up_full)
+    grad_shift_two = jnp.sum(grad_hidden_two, axis=1)
+    grad_scale_two = jnp.sum(grad_hidden_two * normed_two, axis=1)
+    grad_mid = grad_out + norm_back(grad_hidden_two * (1.0 + scale_two), normed_two, inv_two)
+    grad_gate_one = jnp.sum(grad_mid * branch, axis=1)
+    grad_branch = grad_mid * gate_one
+    grad_branch_half = grad_branch.astype(jnp.bfloat16)
+    grad_attended = contract("std,ed->ste", grad_branch_half, proj_full).astype(jnp.bfloat16)
+    proj_local = contract("ste,std->ed", attended, grad_branch_half)
+    grad_heads = split_heads(grad_attended)
+    out_heads = split_heads(attended)
+    row_delta = jnp.transpose(
+        jnp.sum(grad_heads.astype(jnp.float32) * out_heads.astype(jnp.float32), axis=-1), (0, 2, 1)
+    )[..., None]
+    scores_again = contract("sqhd,skhd->shqk", query_heads, key_heads) * scale_dot
+    probs_float = jnp.exp(scores_again - log_total)
+    grad_probs = contract("sqhd,skhd->shqk", grad_heads, value_heads)
+    grad_scores = (probs_float * (grad_probs - row_delta) * scale_dot).astype(jnp.bfloat16)
+    grad_query = contract("shqk,skhd->sqhd", grad_scores, key_heads).reshape(queries.shape)
+    key_partial = contract("shqk,sqhd->skhd", grad_scores, query_heads).reshape(keys_all.shape)
+    value_partial = contract(
+        "shqk,sqhd->skhd", probs_float.astype(jnp.bfloat16), grad_heads
+    ).reshape(values_all.shape)
+    grad_key, grad_value = (
+        lax.psum_scatter(
+            key_partial.astype(jnp.bfloat16), "grp", scatter_dimension=1, tiled=True
+        ).astype(jnp.float32),
+        lax.psum_scatter(
+            value_partial.astype(jnp.bfloat16), "grp", scatter_dimension=1, tiled=True
+        ).astype(jnp.float32),
+    )
+    grad_qkv = jnp.concatenate([grad_query, grad_key, grad_value], axis=-1).astype(jnp.bfloat16)
+    qkv_local = contract("std,ste->de", hidden_one, grad_qkv)
+    attn_bias_local = jnp.concatenate(
+        [
+            jnp.sum(grad_query, axis=(0, 1)),
+            jnp.sum(grad_value, axis=(0, 1)),
+            jnp.sum(grad_branch, axis=(0, 1)),
+            jnp.zeros((FF + D,), jnp.float32),
+        ]
+    )
+    qkv_weight_grad, proj_weight_grad, attn_bias_grad = reduce_bucket(
+        qkv_local, proj_local, attn_bias_local
+    )
+    main_bias_grad = mlp_bias_grad + attn_bias_grad
+    grad_hidden_one = contract("ste,de->std", grad_qkv, qkv_full)
+    grad_shift_one = jnp.sum(grad_hidden_one, axis=1)
+    grad_scale_one = jnp.sum(grad_hidden_one * normed_one, axis=1)
+    tokens_grad = (
+        grad_mid + norm_back(grad_hidden_one * (1.0 + scale_one), normed_one, inv_one)
+    ).astype(jnp.bfloat16)
+    slot_mod_grad = jnp.concatenate(
+        [
+            grad_shift_one,
+            grad_scale_one,
+            grad_gate_one,
+            grad_shift_two,
+            grad_scale_two,
+            grad_gate_two,
+        ],
+        axis=-1,
+    )
+    mod_local = jnp.dot(slot_pick.T, slot_mod_grad, precision=highest)
+    mod_grad = lax.psum(mod_local, ("dp", "grp"))
+    mod_grad_cols = lax.dynamic_slice_in_dim(
+        mod_grad, lax.axis_index("grp") * col_width, col_width, 1
+    )
+    ada_weight_grad = jnp.dot(silu_cond.T, mod_grad_cols, precision=highest)
+    ada_offset_grad = jnp.sum(mod_grad_cols, axis=0)
+    cond_partial = jnp.dot(mod_grad_cols, ada_weight.T, precision=highest)
+    cond_total = lax.psum(cond_partial, "grp")
+    sigmoid_cond = jax.nn.sigmoid(condition)
+    condition_grad = cond_total * sigmoid_cond * (1.0 + condition * (1.0 - sigmoid_cond))
+    data_count = lax.axis_size("dp")
+    square_sums = lax.psum(
+        (
+            jnp.sum(ada_weight_grad * ada_weight_grad),
+            jnp.sum(ada_offset_grad * ada_offset_grad) / data_count,
+            jnp.sum(qkv_weight_grad * qkv_weight_grad),
+            jnp.sum(proj_weight_grad * proj_weight_grad),
+            jnp.sum(up_weight_grad * up_weight_grad),
+            jnp.sum(down_weight_grad * down_weight_grad),
+            jnp.sum(main_bias_grad * main_bias_grad),
+        ),
+        ("dp", "grp"),
+    )
+    entry_counts = (D * 6 * D, 6 * D, D * 3 * HW, HW * D, D * FF, FF * D, 2 * HW + 2 * D + FF)
+    results = []
+    for index_param, (weight, first_mom, second_mom, gradient) in enumerate(
+        (
+            (ada_weight, ada_weight_mean, ada_weight_square, ada_weight_grad),
+            (ada_offset, ada_offset_mean, ada_offset_square, ada_offset_grad),
+            (qkv_weight, qkv_weight_mean, qkv_weight_square, qkv_weight_grad),
+            (proj_weight, proj_weight_mean, proj_weight_square, proj_weight_grad),
+            (up_weight, up_weight_mean, up_weight_square, up_weight_grad),
+            (down_weight, down_weight_mean, down_weight_square, down_weight_grad),
+            (main_bias, main_bias_mean, main_bias_square, main_bias_grad),
+        )
+    ):
+        factor = clip_from(square_sums[index_param], entry_counts[index_param])
+        weight_new, first_new, second_new = adam_update(
+            weight, first_mom, second_mom, gradient, factor
+        )
+        results.append((gradient, weight_new, first_new, second_new))
+    return (
+        block_out,
+        tokens_grad,
+        condition_grad,
+        results[0][0],
+        results[0][1],
+        results[0][2],
+        results[0][3],
+        results[1][0],
+        results[1][1],
+        results[1][2],
+        results[1][3],
+        results[2][0],
+        results[2][1],
+        results[2][2],
+        results[2][3],
+        results[3][0],
+        results[3][1],
+        results[3][2],
+        results[3][3],
+        results[4][0],
+        results[4][1],
+        results[4][2],
+        results[4][3],
+        results[5][0],
+        results[5][1],
+        results[5][2],
+        results[5][3],
+        results[6][0],
+        results[6][1],
+        results[6][2],
+        results[6][3],
+    )
+
+
 def solution(mesh):
+    small = mesh.shape["dp"] == 16 and mesh.shape["grp"] == 2
     return jax.shard_map(
-        local,
+        local if small else local_general,
         mesh=mesh,
         in_specs=(
             P("dp", "grp", None),

time: 1620 us -> 793 us (0.49)
  waiting for transfers between devices: 1090 us -> 295 us
  blocking collectives: 213 us -> 0 us
  other arithmetic: 42.9 us -> 133 us
  starting transfers between devices: 1.05 us -> 58.3 us
  local copies, waits for them, and re-layouts: 65.2 us -> 103 us
    reduce_scatter x5 -> x0, waiting for transfers between devices: 381 us -> none  [the longest x1 188 us: reduce_bucket(): lax.psum_scatter(first_grad.astype(jnp.bfloat16), 'dp', scatter_dimension...]
    all_gather x6 -> x0, waiting for transfers between devices: 306 us -> none  [the longest x1 128 us: local(): lax.all_gather(up_part, 'dp', axis=0, tiled=True)]
    ppermute x0 -> x65, waiting for transfers between devices: none -> 295 us  [the longest x48 290 us: trade(): lax.ppermute(values, 'dp', [(at, at ^ 2 ** bit) for at in range(size)])]
    psum x2 -> x0, waiting for transfers between devices: 228 us -> none  [the longest x1 132 us: local(): mod_grad = lax.psum(mod_local, ('dp', 'grp'))]
    unnamed x27 -> x0, waiting for transfers between devices: 179 us -> none
    unnamed x3 -> x0, blocking collectives: 159 us -> none
    ppermute x0 -> x65, starting transfers between devices: none -> 58.3 us  [the longest x48 55.1 us: trade(): lax.ppermute(values, 'dp', [(at, at ^ 2 ** bit) for at in range(size)])]
    psum x2 -> x0, blocking collectives: 44.8 us -> none  [the longest x1 41.3 us: local(): lax.psum((jnp.sum(ada_weight_grad * ada_weight_grad), jnp.sum(ada_offset_...]
  transfers between devices with their start and end apart: 20 -> 65, of which waited for: 15 -> 32; matrix products, arithmetic and copies ran while one was open for 11% -> 39% of each run, Pallas kernels for 0% -> 0%
where the time goes in v1:
time: 793 us; the launch traced here: 782 us
  waiting for transfers between devices  295 us (37%)
  matrix products  184 us (23%)
  other arithmetic  133 us (17%)
  local copies, waits for them, and re-layouts  103 us (13%)
  starting transfers between devices  58.3 us (7%)
  between operations  8.75 us (1%)
    ppermute x48, waiting for transfers between devices, trade(): lax.ppermute(values, 'dp', [(at, at ^ 2 ** bit) for at in range(size)])  290 us
    dot_general x30, matrix products, contract(): return jnp.einsum(pattern, left, right, preferred_element_type=jnp.float32)  178 us
    ppermute x48, starting transfers between devices, trade(): lax.ppermute(values, 'dp', [(at, at ^ 2 ** bit) for at in range(size)])  55.1 us
    add x16, other arithmetic, scatter_data(): values = kept + trade(sent, bit).astype(jnp.float32)  25.8 us
    convert_element_type x16, other arithmetic, scatter_data(): sent = jnp.where(upper, low, high).astype(wire)  25.7 us
    add x3, local copies, waits for them, and re-layouts, weight_grad(): return scatter_data(own + arrived.astype(jnp.float32), order, jnp.bfloat16)  24.7 us
    unnamed x250, local copies, waits for them, and re-layouts  24.7 us
    another operation x48, other arithmetic, gather_data(): jnp.stack([jnp.where(upper, other, values), jnp.where(upper, values, othe...  24.1 us
  transfers between devices with their start and end apart: 65, of which 32 were waited for; matrix products, arithmetic and copies ran while one was open for 39% of the time, Pallas kernels for 0%

profile of v1, /device:TPU:0, one launch (start us, length us, event | category | flops | bytes accessed | tf_op | source)
XLA Modules:
  0.0 782.0 jit_solution(11041987881735185672)
XLA Ops:
  22.2 8.6 %collective-permute-done.1 = f32[2,1,290]{2,1,0:T(1,128)S(1)} collective-permute-done((f32[2,1,290]{2,1,0:T(1,128)S(1)}, f32[2,1,290]{2,1,0:T(1,128)S(1)}, u32[]{:S(2)}, u32[]{:S(2)}) %collective-permute-start.1) | collective-permute-done | bytes 2352 | tf_op jit(solution)/shard_map/ppermute | solution.py:93
  66.8 12.0 %collective-permute-done.6 = f32[2,2,3456]{2,1,0:T(2,128)S(1)} collective-permute-done((f32[2,2,3456]{2,1,0:T(2,128)S(1)}, f32[2,2,3456]{2,1,0:T(2,128)S(1)}, u32[]{:S(2)}, u32[]{:S(2)}) %collective-permute-start.6) | collective-permute-done | bytes 55328 | tf_op jit(solution)/shard_map/ppermute | solution.py:93
  82.6 7.6 collective-permute-done.7
  96.9 22.6 %collective-permute-done.11 = bf16[2,2,72,1728]{3,2,0,1:T(8,128)(2,1)S(1)} collective-permute-done((bf16[2,2,72,1728]{3,2,0,1:T(8,128)(2,1)S(1)}, bf16[2,2,72,1728]{3,2,0,1:T(8,128)(2,1)S(1)}, u32[]{:S(2)}, u32[]{:S(2)}) %collective-permute-start.11) | collective-permute-done | bytes 995360 | tf_op jit(solution)/shard_map/ppermute | solution.py:93
  131.4 40.2 %collective-permute-done.12 = bf16[2,2,2,72,1728]{4,3,0,1,2:T(8,128)(2,1)S(1)} collective-permute-done((bf16[2,2,2,72,1728]{4,3,0,1,2:T(8,128)(2,1)S(1)}, bf16[2,2,2,72,1728]{4,3,0,1,2:T(8,128)(2,1)S(1)}, u32[]{:S(2)}, u32[]{:S(2)}) %collective-permute-start.12) | collective-permute-done | bytes 1990688 | tf_op jit(solution)/shard_map/ppermute | solution.py:93
  191.4 8.0 %fusion.143 = f32[2,256,1728]{1,2,0:T(8,128)} fusion(bf16[1152,1728,1]{1,0,2:T(8,128)(2,1)} %bitcast.593, bf16[2,256,1152]{1,2,0:T(8,128)(2,1)S(1)} %copy.285, f32[2,1152]{1,0:T(2,128)S(1)} %get-tuple-element.266, f32[2,1152]{1,0:T(2,128)S(1)} %get-tuple-element.267, f32[2,256]{1,0:T(2,128)S(1)} %copy-done.90, f32[2,256]{1,0:T(2,128)S(1)} %broadcast_multiply_fusion.6), kind=kOutput, calls=%fused_computation.391 | convolution fusion | flops 2041970688 | bytes 8722432 | tf_op jit(solution)/shard_map/std,de->ste/dot_general | solution.py:30
  199.3 28.5 %collective-permute-done.25 = bf16[2,2,2,72,2304]{4,3,0,1,2:T(8,128)(2,1)} collective-permute-done((bf16[2,2,2,72,2304]{4,3,0,1,2:T(8,128)(2,1)}, bf16[2,2,2,72,2304]{4,3,0,1,2:T(8,128)(2,1)}, u32[]{:S(2)}, u32[]{:S(2)}) %collective-permute-start.25) | collective-permute-done | bytes 2654240 | tf_op jit(solution)/shard_map/ppermute | solution.py:93
  233.1 18.7 %collective-permute-done.30 = bf16[2,2,2,288,576]{4,3,0,1,2:T(8,128)(2,1)} collective-permute-done((bf16[2,2,2,288,576]{4,3,0,1,2:T(8,128)(2,1)}, bf16[2,2,2,288,576]{4,3,0,1,2:T(8,128)(2,1)}, u32[]{:S(2)}, u32[]{:S(2)}) %collective-permute-start.30) | collective-permute-done | bytes 2654240 | tf_op jit(solution)/shard_map/ppermute | solution.py:93
  258.1 8.3 %copy.316 = bf16[4608,576]{0,1:T(8,128)(2,1)} copy(bf16[4608,576]{1,0:T(8,128)(2,1)} %bitcast.576) | data formatting | bytes 10616832 | tf_op jit(solution)/shard_map/reshape | solution.py:107
  328.4 14.5 %fusion.160 = (f32[4608]{0:T(1024)S(1)}, bf16[2,256,4608]{2,1,0:T(8,128)(2,1)S(1)}) fusion(f32[4608]{0:T(1024)S(1)} %copy-done.82, f32[2,256,2304]{2,1,0:T(8,128)} %copy-done.13, f32[2,256,2304]{2,1,0:T(8,128)} %copy-done.12, f32[2,256,4608]{2,1,0:T(8,128)} %fusion.109, bf16[4608,576]{0,1:T(8,128)(2,1)} %collective-permute-done.31, pred[]{:T(512)S(6)} %eq.18, ...), kind=kOutput, calls=%fused_computation.397 | convolution fusion | flops 2772463104 | bytes 30117888 | tf_op jit(solution)/shard_map/std,fd->stf/dot_general | solution.py:30
  378.5 9.7 %multiply_convert_fusion = bf16[2,16,256,512]{3,2,1,0:T(8,128)(2,1)S(1)} fusion(f32[2,16,256,512]{3,2,1,0:T(8,128)} %copy-done, f32[2,16,256]{2,1,0:T(8,128)S(1)} %bitcast.607, f32[2,16,256]{2,1,0:T(8,128)S(1)} %log_add_fusion, bf16[2,256,16,72]{1,3,2,0:T(8,128)(2,1)} %bitcast.586, bf16[2,512,16,72]{1,3,2,0:T(8,128)(2,1)S(1)} %bitcast.582), kind=kOutput, calls=%fused_computation | convolution fusion | flops 629145600 | bytes 28770304 | tf_op jit(solution)/shard_map/sqhd,skhd->shqk/dot_general | solution.py:30
  397.0 8.8 %bitcast_convert_fusion.1 = (bf16[2,256,16,72]{1,3,2,0:T(8,128)(2,1)}, f32[2,16,72,256]{3,2,1,0:T(8,128)}) fusion(bf16[2,512,16,72]{1,3,2,0:T(8,128)(2,1)} %bitcast.584, bf16[2,16,256,512]{3,2,1,0:T(8,128)(2,1)} %copy-done.1), kind=kOutput, calls=%fused_computation.104 | convolution fusion | flops 604569600 | bytes 14286848 | tf_op jit(solution)/shard_map/shqk,skhd->sqhd/dot_general | solution.py:30
  422.1 8.1 %fusion.1 = bf16[1152,2304]{1,0:T(8,128)(2,1)} fusion(bf16[2,256,1152]{1,2,0:T(8,128)(2,1)} %copy-done.23, pred[]{:T(512)S(6)} %eq.18, bf16[2,256,4608]{2,1,0:T(8,128)(2,1)} %copy-done.102), kind=kOutput, calls=%fused_computation.9 | convolution fusion | flops 2721742848 | bytes 11206657 | tf_op jit(solution)/shard_map/std,stf->df/dot_general | solution.py:30
  496.0 8.8 %collective-permute-done.46 = bf16[2,2,2,72,576]{4,3,2,1,0:T(8,128)(2,1)} collective-permute-done((bf16[2,2,2,72,576]{4,3,2,1,0:T(8,128)(2,1)}, bf16[2,2,2,72,576]{4,3,2,1,0:T(8,128)(2,1)}, u32[]{:S(2)}, u32[]{:S(2)}) %collective-permute-start.46) | collective-permute-done | bytes 663584 | tf_op jit(solution)/shard_map/ppermute | solution.py:93
  524.5 8.2 %convert_add_fusion.1 = f32[1152,1728]{0,1:T(8,128)} fusion(bf16[1152,1728]{0,1:T(8,128)(2,1)} %collective-permute-done.40, bf16[2,256,1152]{1,2,0:T(8,128)(2,1)S(1)} %copy.285, f32[2,1152]{1,0:T(2,128)S(1)} %copy-done.81, f32[2,1152]{1,0:T(2,128)S(1)} %copy-done.74, f32[2,256]{1,0:T(2,128)S(1)} %copy-done.91, f32[2,256]{1,0:T(2,128)S(1)} %broadcast_multiply_fusion.6, ...), kind=kOutput, calls=%fused_computation.23 | convolution fusion | flops 2053914624 | bytes 16685057 | tf_op jit(solution)/shard_map/std,ste->de/dot_general | solution.py:30
  532.7 8.9 %copy.331 = f32[1152,1728]{1,0:T(8,128)} copy(f32[1152,1728]{0,1:T(8,128)} %convert_add_fusion.1) | data formatting | bytes 15925248 | tf_op jit(solution)/shard_map/add | solution.py:154
  548.4 8.9 %convert_add_fusion = f32[1152,2304]{1,0:T(8,128)} fusion(bf16[1152,2304]{1,0:T(8,128)(2,1)} %collective-permute-done.50, bf16[2,256,1152]{1,2,0:T(8,128)(2,1)S(1)} %copy-done.24, pred[]{:T(512)S(6)} %eq.18, bf16[2,256,4608]{2,1,0:T(8,128)(2,1)} %copy-done.102), kind=kOutput, calls=%fused_computation.12 | convolution fusion | flops 2724397056 | bytes 21823488 | tf_op jit(solution)/shard_map/std,stf->df/dot_general | solution.py:30
  569.8 8.8 %bitcast_add_fusion = f32[4608,576]{0,1:T(8,128)} fusion(bf16[4608,576]{0,1:T(8,128)(2,1)} %collective-permute-done.55, bf16[2,256,4608]{2,1,0:T(8,128)(2,1)} %copy-done.10, pred[]{:T(512)S(6)} %eq.18, bf16[2,256,1152]{1,2,0:T(8,128)(2,1)S(1)} %copy-done.47), kind=kOutput, calls=%fused_computation.11 | convolution fusion | flops 2723512320 | bytes 21823488 | tf_op jit(solution)/shard_map/stf,std->fd/dot_general | solution.py:30
  578.7 12.1 %copy.361 = f32[4608,576]{1,0:T(8,128)} copy(f32[4608,576]{0,1:T(8,128)} %bitcast_add_fusion) | data formatting | bytes 21233664 | tf_op jit(solution)/shard_map/add | solution.py:154
  604.4 23.5 %collective-permute-done.51 = bf16[2,2,2,72,2304]{4,3,0,1,2:T(8,128)(2,1)} collective-permute-done((bf16[2,2,2,72,2304]{4,3,0,1,2:T(8,128)(2,1)}, bf16[2,2,2,72,2304]{4,3,0,1,2:T(8,128)(2,1)}, u32[]{:S(2)}, u32[]{:S(2)}) %collective-permute-start.51) | collective-permute-done | bytes 2654240 | tf_op jit(solution)/shard_map/ppermute | solution.py:93
  648.1 16.6 %collective-permute-done.56 = bf16[2,2,2,288,576]{4,3,2,1,0:T(8,128)(2,1)} collective-permute-done((bf16[2,2,2,288,576]{4,3,2,1,0:T(8,128)(2,1)}, bf16[2,2,2,288,576]{4,3,2,1,0:T(8,128)(2,1)}, u32[]{:S(2)}, u32[]{:S(2)}) %collective-permute-start.56) | collective-permute-done | bytes 2654240 | tf_op jit(solution)/shard_map/ppermute | solution.py:93
  676.1 12.5 %collective-permute-done.52 = bf16[2,2,72,2304]{3,2,0,1:T(8,128)(2,1)} collective-permute-done((bf16[2,2,72,2304]{3,2,0,1:T(8,128)(2,1)}, bf16[2,2,72,2304]{3,2,0,1:T(8,128)(2,1)}, u32[]{:S(2)}, u32[]{:S(2)}) %collective-permute-start.52) | collective-permute-done | bytes 1327136 | tf_op jit(solution)/shard_map/ppermute | solution.py:93
  699.4 14.1 %collective-permute-done.53 = bf16[2,72,2304]{2,1,0:T(8,128)(2,1)S(1)} collective-permute-done((bf16[2,72,2304]{2,1,0:T(8,128)(2,1)S(1)}, bf16[2,72,2304]{2,1,0:T(8,128)(2,1)S(1)}, u32[]{:S(2)}, u32[]{:S(2)}) %collective-permute-start.53) | collective-permute-done | bytes 663584 | tf_op jit(solution)/shard_map/ppermute | solution.py:93
  714.5 13.6 %collective-permute-done.58 = bf16[2,288,576]{2,1,0:T(8,128)(2,1)S(1)} collective-permute-done((bf16[2,288,576]{2,1,0:T(8,128)(2,1)S(1)}, bf16[2,288,576]{2,1,0:T(8,128)(2,1)S(1)}, u32[]{:S(2)}, u32[]{:S(2)}) %collective-permute-start.58) | collective-permute-done | bytes 663584 | tf_op jit(solution)/shard_map/ppermute | solution.py:93
  (590 shorter events, 441.7 us)
Async XLA Ops:
  8.0 53.9 %collective-permute-start.9 = (bf16[72,1728]{1,0:T(8,128)(2,1)}, bf16[72,1728]{1,0:T(8,128)(2,1)}, u32[]{:S(2)}, u32[]{:S(2)}) collective-permute-start(bf16[72,1728]{1,0:T(8,128)(2,1)} %convert_element_type.278), channel_id=1, source_target_pairs={{0,16},{2,18},{4,20},{6,22},{8,24},{10,26},{12,28},{14,30},{16,0},... | collective-permute-start | bytes 746504 | tf_op jit(solution)/shard_map/ppermute | solution.py:93
  14.3 49.1 %collective-permute-start.22 = (bf16[72,2304]{1,0:T(8,128)(2,1)}, bf16[72,2304]{1,0:T(8,128)(2,1)}, u32[]{:S(2)}, u32[]{:S(2)}) collective-permute-start(bf16[72,2304]{1,0:T(8,128)(2,1)} %convert_element_type.286), channel_id=1, source_target_pairs={{0,16},{2,18},{4,20},{6,22},{8,24},{10,26},{12,28},{14,30},{16,0},... | collective-permute-start | bytes 995336 | tf_op jit(solution)/shard_map/ppermute | solution.py:93
  15.1 66.4 %collective-permute-start.27 = (bf16[288,576]{1,0:T(8,128)(2,1)}, bf16[288,576]{1,0:T(8,128)(2,1)}, u32[]{:S(2)}, u32[]{:S(2)}) collective-permute-start(bf16[288,576]{1,0:T(8,128)(2,1)} %convert_element_type.288), channel_id=1, source_target_pairs={{0,16},{2,18},{4,20},{6,22},{8,24},{10,26},{12,28},{14,30},{16,0},... | collective-permute-start | bytes 995336 | tf_op jit(solution)/shard_map/ppermute | solution.py:93
  60.3 60.1 %collective-permute-start.19 = (bf16[2,2,72,576]{3,2,0,1:T(8,128)(2,1)S(1)}, bf16[2,2,72,576]{3,2,0,1:T(8,128)(2,1)S(1)}, u32[]{:S(2)}, u32[]{:S(2)}) collective-permute-start(bf16[2,2,72,576]{3,2,0,1:T(8,128)(2,1)S(1)} %pad_maximum_fusion.20), channel_id=1, source_target_pairs={{0,2},{2,0},{4,6},{6,4},{8,10},{10,8},{12,14},{14,12},{16,18},{18,... | collective-permute-start | bytes 995336 | tf_op jit(solution)/shard_map/ppermute | solution.py:93
  119.8 51.7 %collective-permute-start.12 = (bf16[2,2,2,72,1728]{4,3,0,1,2:T(8,128)(2,1)S(1)}, bf16[2,2,2,72,1728]{4,3,0,1,2:T(8,128)(2,1)S(1)}, u32[]{:S(2)}, u32[]{:S(2)}) collective-permute-start(bf16[2,2,2,72,1728]{4,3,0,1,2:T(8,128)(2,1)S(1)} %pad_maximum_fusion.7), channel_id=1, source_target_pairs={{0,2},{2,0},{4,6},{6,4},{8,10},{10,8},{12,14},{14,12},{16,18},{18,... | collective-permute-start | bytes 5971976 | tf_op jit(solution)/shard_map/ppermute | solution.py:93
  121.5 64.2 %collective-permute-start.20 = (bf16[2,2,2,72,576]{4,3,0,1,2:T(8,128)(2,1)}, bf16[2,2,2,72,576]{4,3,0,1,2:T(8,128)(2,1)}, u32[]{:S(2)}, u32[]{:S(2)}) collective-permute-start(bf16[2,2,2,72,576]{4,3,0,1,2:T(8,128)(2,1)} %pad_maximum_fusion.15), channel_id=1, source_target_pairs={{0,4},{2,6},{4,0},{6,2},{8,12},{10,14},{12,8},{14,10},{16,20},{18,... | collective-permute-start | bytes 1990664 | tf_op jit(solution)/shard_map/ppermute | solution.py:93
  123.5 57.4 %collective-permute-start.29 = (bf16[2,2,288,576]{3,2,0,1:T(8,128)(2,1)S(1)}, bf16[2,2,288,576]{3,2,0,1:T(8,128)(2,1)}, u32[]{:S(2)}, u32[]{:S(2)}) collective-permute-start(bf16[2,2,288,576]{3,2,0,1:T(8,128)(2,1)S(1)} %pad_maximum_fusion.11), channel_id=1, source_target_pairs={{0,4},{2,6},{4,0},{6,2},{8,12},{10,14},{12,8},{14,10},{16,20},{18,... | collective-permute-start | bytes 3981320 | tf_op jit(solution)/shard_map/ppermute | solution.py:93
  130.9 96.9 %collective-permute-start.25 = (bf16[2,2,2,72,2304]{4,3,0,1,2:T(8,128)(2,1)}, bf16[2,2,2,72,2304]{4,3,0,1,2:T(8,128)(2,1)}, u32[]{:S(2)}, u32[]{:S(2)}) collective-permute-start(bf16[2,2,2,72,2304]{4,3,0,1,2:T(8,128)(2,1)} %pad_maximum_fusion.4), channel_id=1, source_target_pairs={{0,4},{2,6},{4,0},{6,2},{8,12},{10,14},{12,8},{14,10},{16,20},{18,... | collective-permute-start | bytes 7962632 | tf_op jit(solution)/shard_map/ppermute | solution.py:93
  180.9 85.5 %collective-permute-start.13 = (bf16[1152,1728]{0,1:T(8,128)(2,1)}, bf16[1152,1728]{0,1:T(8,128)(2,1)}, u32[]{:S(2)}, u32[]{:S(2)}) collective-permute-start(bf16[1152,1728]{0,1:T(8,128)(2,1)} %copy.302), channel_id=1, source_target_pairs={{0,1},{1,0},{2,3},{3,2},{4,5},{5,4},{6,7},{7,6},{8,9},{9,8},{10,11... | collective-permute-start | bytes 11943944 | tf_op jit(solution)/shard_map/ppermute | solution.py:80
  185.1 66.6 %collective-permute-start.30 = (bf16[2,2,2,288,576]{4,3,0,1,2:T(8,128)(2,1)}, bf16[2,2,2,288,576]{4,3,0,1,2:T(8,128)(2,1)}, u32[]{:S(2)}, u32[]{:S(2)}) collective-permute-start(bf16[2,2,2,288,576]{4,3,0,1,2:T(8,128)(2,1)} %pad_maximum_fusion.3), channel_id=1, source_target_pairs={{0,2},{2,0},{4,6},{6,4},{8,10},{10,8},{12,14},{14,12},{16,18},{18,... | collective-permute-start | bytes 7962632 | tf_op jit(solution)/shard_map/ppermute | solution.py:93
  191.1 103.5 %collective-permute-start.21 = (bf16[1152,576]{0,1:T(8,128)(2,1)}, bf16[1152,576]{0,1:T(8,128)(2,1)}, u32[]{:S(2)}, u32[]{:S(2)}) collective-permute-start(bf16[1152,576]{0,1:T(8,128)(2,1)} %copy.309), channel_id=1, source_target_pairs={{0,1},{1,0},{2,3},{3,2},{4,5},{5,4},{6,7},{7,6},{8,9},{9,8},{10,11... | collective-permute-start | bytes 3981320 | tf_op jit(solution)/shard_map/ppermute | solution.py:80
  233.1 79.7 %collective-permute-start.26 = (bf16[1152,2304]{1,0:T(8,128)(2,1)}, bf16[1152,2304]{1,0:T(8,128)(2,1)}, u32[]{:S(2)}, u32[]{:S(2)}) collective-permute-start(bf16[1152,2304]{1,0:T(8,128)(2,1)} %bitcast.71), channel_id=1, source_target_pairs={{0,1},{1,0},{2,3},{3,2},{4,5},{5,4},{6,7},{7,6},{8,9},{9,8},{10,11... | collective-permute-start | bytes 15925256 | tf_op jit(solution)/shard_map/ppermute | solution.py:80
  266.4 62.0 %collective-permute-start.31 = (bf16[4608,576]{0,1:T(8,128)(2,1)}, bf16[4608,576]{0,1:T(8,128)(2,1)}, u32[]{:S(2)}, u32[]{:S(2)}) collective-permute-start(bf16[4608,576]{0,1:T(8,128)(2,1)} %copy.316), channel_id=1, source_target_pairs={{0,1},{1,0},{2,3},{3,2},{4,5},{5,4},{6,7},{7,6},{8,9},{9,8},{10,11... | collective-permute-start | bytes 15925256 | tf_op jit(solution)/shard_map/ppermute | solution.py:80
  421.9 53.3 %collective-permute-start.45 = (bf16[1152,576]{0,1:T(8,128)(2,1)}, bf16[1152,576]{0,1:T(8,128)(2,1)}, u32[]{:S(2)}, u32[]{:S(2)}) collective-permute-start(bf16[1152,576]{0,1:T(8,128)(2,1)} %fusion.30), channel_id=1, source_target_pairs={{0,1},{1,0},{2,3},{3,2},{4,5},{5,4},{6,7},{7,6},{8,9},{9,8},{10,11... | collective-permute-start | bytes 3981320 | tf_op jit(solution)/shard_map/ppermute | solution.py:80
  430.2 118.1 %collective-permute-start.50 = (bf16[1152,2304]{1,0:T(8,128)(2,1)}, bf16[1152,2304]{1,0:T(8,128)(2,1)}, u32[]{:S(2)}, u32[]{:S(2)}) collective-permute-start(bf16[1152,2304]{1,0:T(8,128)(2,1)} %fusion.1), channel_id=1, source_target_pairs={{0,1},{1,0},{2,3},{3,2},{4,5},{5,4},{6,7},{7,6},{8,9},{9,8},{10,11... | collective-permute-start | bytes 15925256 | tf_op jit(solution)/shard_map/ppermute | solution.py:80
  437.8 132.0 %collective-permute-start.55 = (bf16[4608,576]{0,1:T(8,128)(2,1)}, bf16[4608,576]{0,1:T(8,128)(2,1)}, u32[]{:S(2)}, u32[]{:S(2)}) collective-permute-start(bf16[4608,576]{0,1:T(8,128)(2,1)} %bitcast_convert_fusion), channel_id=1, source_target_pairs={{0,1},{1,0},{2,3},{3,2},{4,5},{5,4},{6,7},{7,6},{8,9},{9,8},{10,11... | collective-permute-start | bytes 15925256 | tf_op jit(solution)/shard_map/ppermute | solution.py:80
  473.2 51.3 %collective-permute-start.40 = (bf16[1152,1728]{0,1:T(8,128)(2,1)}, bf16[1152,1728]{0,1:T(8,128)(2,1)}, u32[]{:S(2)}, u32[]{:S(2)}) collective-permute-start(bf16[1152,1728]{0,1:T(8,128)(2,1)} %fusion.8), channel_id=1, source_target_pairs={{0,1},{1,0},{2,3},{3,2},{4,5},{5,4},{6,7},{7,6},{8,9},{9,8},{10,11... | collective-permute-start | bytes 11943944 | tf_op jit(solution)/shard_map/ppermute | solution.py:80
  522.9 45.6 %collective-permute-start.49 = (bf16[72,576]{1,0:T(8,128)(2,1)S(1)}, bf16[72,576]{1,0:T(8,128)(2,1)S(1)}, u32[]{:S(2)}, u32[]{:S(2)}) collective-permute-start(bf16[72,576]{1,0:T(8,128)(2,1)S(1)} %fusion.108), channel_id=1, source_target_pairs={{0,16},{2,18},{4,20},{6,22},{8,24},{10,26},{12,28},{14,30},{16,0},... | collective-permute-start | bytes 248840 | tf_op jit(solution)/shard_map/ppermute | solution.py:93
  546.8 51.2 %collective-permute-start.41 = (bf16[2,2,2,72,1728]{4,3,2,1,0:T(8,128)(2,1)}, bf16[2,2,2,72,1728]{4,3,2,1,0:T(8,128)(2,1)}, u32[]{:S(2)}, u32[]{:S(2)}) collective-permute-start(bf16[2,2,2,72,1728]{4,3,2,1,0:T(8,128)(2,1)} %fusion.57), channel_id=1, source_target_pairs={{0,2},{2,0},{4,6},{6,4},{8,10},{10,8},{12,14},{14,12},{16,18},{18,... | collective-permute-start | bytes 5971976 | tf_op jit(solution)/shard_map/ppermute | solution.py:93
  567.0 60.8 %collective-permute-start.51 = (bf16[2,2,2,72,2304]{4,3,0,1,2:T(8,128)(2,1)}, bf16[2,2,2,72,2304]{4,3,0,1,2:T(8,128)(2,1)}, u32[]{:S(2)}, u32[]{:S(2)}) collective-permute-start(bf16[2,2,2,72,2304]{4,3,0,1,2:T(8,128)(2,1)} %fusion.41), channel_id=1, source_target_pairs={{0,4},{2,6},{4,0},{6,2},{8,12},{10,14},{12,8},{14,10},{16,20},{18,... | collective-permute-start | bytes 7962632 | tf_op jit(solution)/shard_map/ppermute | solution.py:93
  597.5 67.1 %collective-permute-start.56 = (bf16[2,2,2,288,576]{4,3,2,1,0:T(8,128)(2,1)}, bf16[2,2,2,288,576]{4,3,2,1,0:T(8,128)(2,1)}, u32[]{:S(2)}, u32[]{:S(2)}) collective-permute-start(bf16[2,2,2,288,576]{4,3,2,1,0:T(8,128)(2,1)} %fusion.32), channel_id=1, source_target_pairs={{0,2},{2,0},{4,6},{6,4},{8,10},{10,8},{12,14},{14,12},{16,18},{18,... | collective-permute-start | bytes 7962632 | tf_op jit(solution)/shard_map/ppermute | solution.py:93
  603.9 41.8 %collective-permute-start.42 = (bf16[2,2,72,1728]{3,2,1,0:T(8,128)(2,1)}, bf16[2,2,72,1728]{3,2,1,0:T(8,128)(2,1)}, u32[]{:S(2)}, u32[]{:S(2)}) collective-permute-start(bf16[2,2,72,1728]{3,2,1,0:T(8,128)(2,1)} %fusion.74), channel_id=1, source_target_pairs={{0,4},{2,6},{4,0},{6,2},{8,12},{10,14},{12,8},{14,10},{16,20},{18,... | collective-permute-start | bytes 2985992 | tf_op jit(solution)/shard_map/ppermute | solution.py:93
  638.5 50.0 %collective-permute-start.52 = (bf16[2,2,72,2304]{3,2,0,1:T(8,128)(2,1)}, bf16[2,2,72,2304]{3,2,0,1:T(8,128)(2,1)}, u32[]{:S(2)}, u32[]{:S(2)}) collective-permute-start(bf16[2,2,72,2304]{3,2,0,1:T(8,128)(2,1)} %fusion.67), channel_id=1, source_target_pairs={{0,2},{2,0},{4,6},{6,4},{8,10},{10,8},{12,14},{14,12},{16,18},{18,... | collective-permute-start | bytes 3981320 | tf_op jit(solution)/shard_map/ppermute | solution.py:93
  674.6 54.0 %collective-permute-start.44 = (bf16[72,1728]{1,0:T(8,128)(2,1)S(1)}, bf16[72,1728]{1,0:T(8,128)(2,1)S(1)}, u32[]{:S(2)}, u32[]{:S(2)}) collective-permute-start(bf16[72,1728]{1,0:T(8,128)(2,1)S(1)} %fusion.95), channel_id=1, source_target_pairs={{0,16},{2,18},{4,20},{6,22},{8,24},{10,26},{12,28},{14,30},{16,0},... | collective-permute-start | bytes 746504 | tf_op jit(solution)/shard_map/ppermute | solution.py:93
  (163 other events, 2904.6 us)
